TPU v7x, 32 devices: a whole 2x2x4 slice. The times are simulated.
32 devices in a mesh: req: 16 (over z, y, x), tp: 2 (over core).
Axes of the slice: x: 2, y: 2, z: 4, core: 2. Of those that a mesh axis runs over, the one named last changes fastest.
Arguments:
- queries: bfloat16 [16, 28, 4096], P('req', None, 'tp'), may hold values from -25 to 25
- tree_kv: bfloat16 [16, 28, 2048], P('req', None, 'tp'), may hold values from -4 to 4
- tree_parent: int32 [16, 28], P('req'), may hold values from -1 to 26, as said below
- accepted_path: int32 [16, 8], replicated, may hold values from -1 to 27, as said below
- cache_kv: bfloat16 [48, 256, 2048], P('req', None, 'tp'), may hold values from -6 to 6
- piece_owner: int32 [48, 2], P('req'), may hold values from -1 to 15, as said below
- cache_len: int32 [16], replicated, may hold values from 1 to 1016, as said below
- out_weight: bfloat16 [4096, 4096], P('tp', 'req'), may hold values from -0.09375 to 0.09375
Outputs:
- mixed: bfloat16 [16, 28, 4096], P('tp', None, 'req')
- cache_out: bfloat16 [48, 256, 2048], P('req', None, 'tp')
Inputs may be any that keep to these rules, and one draw needn't show every extreme that they name: tree_parent[r, 0] = -1 and 0 <= tree_parent[r, i] < i for i >= 1; tokens 1 to 7 have parent i - 1. accepted_path[r] lists, root first, the tokens on the path from token 0 to some token of request r's tree, then -1 entries; it holds 1 to 8 tokens, and 8 for some request. piece_owner[s] = (r, p) means slot s holds cache rows p * 256 to p * 256 + 255 of request r; (-1, -1) marks an unused slot. For each request r the pieces 0 to (cache_len[r] + 7) // 256 stand in exactly one slot each, and no other pieces do. cache_len[r] + 8 <= 1024.
All inputs are finite; a program needn't handle non-finite values.
Results may differ from a plain program's by a relative error of at most 0.02.
Values may be sent and summed in bfloat16 or wider, within the bound.
A program may use at most 64 MiB of HBM per device.

v0:
```python
import math

import jax
import jax.numpy as jnp
from jax import lax
from jax.sharding import PartitionSpec as P

HD = 128


NEG = -1e30


def ancestors(parent):
    tree_size = parent.shape[-1]
    node_ids = lax.broadcasted_iota(jnp.int32, (tree_size, tree_size), 1)
    parent_hot = (parent[..., :, None] == node_ids).astype(jnp.float32)
    reached = jnp.minimum(parent_hot + jnp.eye(tree_size, dtype=jnp.float32), 1.0)
    for rounds in range(max(1, (tree_size - 1).bit_length())):
        reached = jnp.minimum(
            jnp.einsum("rij,rjk->rik", reached, reached, precision=lax.Precision.HIGHEST), 1.0
        )
    return reached


def shards(
    queries, tree_kv, tree_parent, accepted_path, cache_kv, piece_owner, cache_len, out_weight
):
    kvheads_local = tree_kv.shape[-1] // (2 * HD)
    heads_local = queries.shape[-1] // HD
    group_size = heads_local // kvheads_local
    tree_size = queries.shape[1]
    slot_count = cache_kv.shape[0]
    piece_rows = cache_kv.shape[1]
    depth_most = accepted_path.shape[1]
    scaling = 1.0 / math.sqrt(HD)
    every_query = lax.all_gather(queries, "req", axis=0, tiled=True)
    req_total = every_query.shape[0]
    owner_req = piece_owner[:, 0]
    owner_piece = piece_owner[:, 1]
    safe_req = jnp.maximum(owner_req, 0)
    slot_query = every_query[safe_req].reshape(slot_count, tree_size, kvheads_local, group_size, HD)
    stored = cache_kv.reshape(slot_count, piece_rows, kvheads_local, 2, HD)
    row_pos = owner_piece[:, None] * piece_rows + lax.broadcasted_iota(
        jnp.int32, (slot_count, piece_rows), 1
    )
    visible = (owner_req >= 0)[:, None] & (row_pos < cache_len[safe_req][:, None])
    wide_mask = visible[:, None, None, None, :]
    scores = (
        jnp.einsum(
            "stkgd,spkd->stkgp", slot_query, stored[:, :, :, 0], preferred_element_type=jnp.float32
        )
        * scaling
    )
    scores = jnp.where(wide_mask, scores, NEG)
    slot_peak = jnp.max(scores, -1)
    expo = jnp.where(wide_mask, jnp.exp(scores - slot_peak[..., None]), 0.0)
    slot_den = jnp.sum(expo, -1)
    weights = expo.astype(jnp.bfloat16)
    slot_num = jnp.einsum(
        "stkgp,spkd->stkgd", weights, stored[:, :, :, 1], preferred_element_type=jnp.float32
    )
    request_ids = lax.broadcasted_iota(jnp.int32, (req_total, slot_count), 0)
    member = (owner_req[None, :] == request_ids)[:, :, None, None, None]
    req_peak = jnp.max(jnp.where(member, slot_peak[None], NEG), axis=1)
    factor = jnp.where(
        member, jnp.exp(jnp.where(member, slot_peak[None] - req_peak[:, None], 0.0)), 0.0
    )
    req_den = jnp.sum(factor * slot_den[None], axis=1)
    req_num = jnp.einsum("rstkg,stkgd->rtkgd", factor, slot_num, precision=lax.Precision.HIGHEST)
    peak_table = req_peak.reshape(req_total, tree_size, heads_local)
    den_table = req_den.reshape(req_total, tree_size, heads_local)
    num_table = req_num.reshape(req_total, tree_size, heads_local * HD)
    own_index = lax.axis_index("req")
    got_peak, got_den, got_num = (
        lax.all_to_all(
            peak_table.astype(jnp.bfloat16), "req", split_axis=0, concat_axis=0, tiled=True
        ).astype(peak_table.dtype),
        lax.all_to_all(
            den_table.astype(jnp.bfloat16), "req", split_axis=0, concat_axis=0, tiled=True
        ).astype(den_table.dtype),
        lax.all_to_all(
            num_table.astype(jnp.bfloat16), "req", split_axis=0, concat_axis=0, tiled=True
        ).astype(num_table.dtype),
    )
    cache_peak = jnp.max(got_peak, axis=0)
    source_scale = jnp.exp(got_peak - cache_peak[None])
    cache_den = jnp.sum(source_scale * got_den, axis=0)
    got_rows = got_num.reshape(got_num.shape[0], tree_size, heads_local, HD)
    cache_num = jnp.sum(source_scale[..., None] * got_rows, axis=0)
    reached = ancestors(tree_parent)[0]
    home_query = queries[0].reshape(tree_size, kvheads_local, group_size, HD)
    fresh = tree_kv[0].reshape(tree_size, kvheads_local, 2, HD)
    tree_mask = reached[:, None, None, :] > 0.5
    tree_scores = (
        jnp.einsum("ikgd,jkd->ikgj", home_query, fresh[:, :, 0], preferred_element_type=jnp.float32)
        * scaling
    )
    tree_scores = jnp.where(tree_mask, tree_scores, NEG)
    tree_peak = jnp.max(tree_scores, -1)
    tree_exp = jnp.where(tree_mask, jnp.exp(tree_scores - tree_peak[..., None]), 0.0)
    tree_den = jnp.sum(tree_exp, -1).reshape(tree_size, heads_local)
    tree_num = jnp.einsum(
        "ikgj,jkd->ikgd",
        tree_exp.astype(jnp.bfloat16),
        fresh[:, :, 1],
        preferred_element_type=jnp.float32,
    )
    tree_num = tree_num.reshape(tree_size, heads_local, HD)
    tree_peak = tree_peak.reshape(tree_size, heads_local)
    total_peak = jnp.maximum(cache_peak, tree_peak)
    cache_scale = jnp.exp(cache_peak - total_peak)
    tree_scale = jnp.exp(tree_peak - total_peak)
    denom = cache_den * cache_scale + tree_den * tree_scale
    numer = cache_num * cache_scale[..., None] + tree_num * tree_scale[..., None]
    attention = (
        (numer / denom[..., None]).reshape(1, tree_size, heads_local * HD).astype(jnp.bfloat16)
    )
    piece = lax.all_gather(attention, "req", axis=0, tiled=True)
    flat_rows = piece.reshape(piece.shape[0] * piece.shape[1], piece.shape[2])
    product = jnp.dot(flat_rows, out_weight, preferred_element_type=jnp.float32)
    terms = product.reshape(piece.shape[0], piece.shape[1], out_weight.shape[1])
    mixed = lax.psum_scatter(terms.astype(jnp.bfloat16), "tp", scatter_dimension=0, tiled=True)
    own_path = lax.dynamic_index_in_dim(accepted_path, own_index, 0, keepdims=False)
    picked = tree_kv[0][jnp.maximum(own_path, 0)]
    picked = jnp.where((own_path >= 0)[:, None], picked, jnp.zeros_like(picked))
    all_rows = lax.all_gather(picked[None], "req", axis=0, tiled=True)
    counts = jnp.sum((accepted_path >= 0).astype(jnp.int32), axis=1)
    offset = row_pos - cache_len[safe_req][:, None]
    writing = (owner_req >= 0)[:, None] & (offset >= 0) & (offset < counts[safe_req][:, None])
    slot_rows = all_rows[safe_req]
    chosen = jnp.take_along_axis(slot_rows, jnp.clip(offset, 0, depth_most - 1)[:, :, None], axis=1)
    cache_out = jnp.where(writing[:, :, None], chosen, cache_kv)
    return (mixed, cache_out)


def solution(mesh):
    return jax.shard_map(
        shards,
        mesh=mesh,
        in_specs=(
            P("req", None, "tp"),
            P("req", None, "tp"),
            P("req", None),
            P(),
            P("req", None, "tp"),
            P("req", None),
            P(),
            P("tp", "req"),
        ),
        out_specs=(P("tp", None, "req"), P("req", None, "tp")),
        check_vma=False,
    )
```

profile of v0, /device:TPU:0, one launch (start us, length us, event | category | flops | bytes accessed | tf_op | source)
XLA Modules:
  0.0 248.6 jit_solution(9096392429616548951)
XLA Ops:
  7.2 0.7 all-gather.3.cloned.1.call-update
  7.9 0.8 slice_bitcast_fusion.4
  8.7 1.3 gather_fusion
  10.0 0.7 convert_reduce_fusion
  10.7 0.6 gather_fusion.2
  11.3 2.6 %copy.106 = bf16[3,256,1024]{1,2,0:T(8,128)(2,1)} copy(bf16[3,256,1024]{2,1,0:T(8,128)(2,1)} %param.12) | data formatting | bytes 3145728 | tf_op args[4]
  14.0 0.7 fusion.37
  14.7 59.5 %all-gather.3.cloned.1.call-done = bf16[16,28,2048]{2,1,0:T(8,128)(2,1)} async-done(((bf16[1,28,2048]{2,1,0:T(8,128)(2,1)}), bf16[16,28,2048]{2,1,0:T(8,128)(2,1)}) %all-gather.3.cloned.1.call-update) | async-done | bytes 1835024 | tf_op jit(solution)/shard_map/all_gather | solution.py:37
  74.2 2.2 gather_fusion.1
  76.6 1.6 bitcast_reduce_fusion
  78.2 0.2 copy.109
  78.4 0.6 fusion.2
  79.0 0.2 copy.127
  79.3 0.8 select_reduce_fusion
  80.1 1.2 multiply_reduce_fusion.1
  81.3 0.2 copy.128
  81.5 0.7 reshape.596
  82.2 4.3 %all-to-all-start.2 = ((bf16[16,2,224]{2,1,0:T(2,128)(2,1)}), bf16[16,2,224]{2,1,0:T(2,128)(2,1)S(1)}, u32[]{:S(2)}, u32[]{:S(2)}) async-start(bf16[16,2,224]{2,1,0:T(2,128)(2,1)} %reshape.596), calls=%async_computation.2 | async-start | bytes 32768 | tf_op jit(solution)/shard_map/all_to_all | solution.py:79
  86.5 2.5 convolution_bitcast_fusion
  89.0 0.2 copy.110
  89.2 0.7 reshape.594
  89.9 3.9 %all-to-all-done.2 = bf16[16,2,224]{2,1,0:T(2,128)(2,1)S(1)} async-done(((bf16[16,2,224]{2,1,0:T(2,128)(2,1)}), bf16[16,2,224]{2,1,0:T(2,128)(2,1)S(1)}, u32[]{:S(2)}, u32[]{:S(2)}) %all-to-all-start.2) | async-done | bytes 14368 | tf_op jit(solution)/shard_map/all_to_all | solution.py:79
  93.8 3.5 %all-to-all-start = ((bf16[16,2,224]{2,1,0:T(2,128)(2,1)}), bf16[16,2,224]{2,1,0:T(2,128)(2,1)S(1)}, u32[]{:S(2)}, u32[]{:S(2)}) async-start(bf16[16,2,224]{2,1,0:T(2,128)(2,1)} %reshape.594), calls=%async_computation | async-start | bytes 32768 | tf_op jit(solution)/shard_map/all_to_all | solution.py:76
  97.3 7.9 %convert_bitcast_fusion = bf16[16,28,4,4,128]{4,0,3,2,1:T(8,128)(2,1)S(1)} fusion(f32[3,28,4,4,128]{4,1,3,2,0:T(8,128)} %convolution_bitcast_fusion, f32[16,28,4,4]{0,3,2,1:T(4,128)S(1)} %select_reduce_fusion, f32[3,28,4,4]{0,3,2,1:T(4,128)S(1)} %copy.109, pred[16,3]{0,1:T(4,128)(4,1)S(1)} %iota_compare_fusion), kind=kOutput, calls=%fused_computation.7 | convolution fusion | flops 34012160 | bytes 2557232 | tf_op jit(solution)/shard_map/rstkg,stkgd->rtkgd/dot_general | solution.py:70
  105.2 0.9 copy.137
  106.1 2.1 reshape.591
  108.3 0.6 copy-done.6
  108.9 6.9 %all-to-all-start.1 = ((bf16[16,28,2048]{2,1,0:T(8,128)(2,1)}), bf16[16,28,2048]{2,1,0:T(8,128)(2,1)S(1)}, u32[]{:S(2)}, u32[]{:S(2)}) async-start(bf16[16,28,2048]{2,1,0:T(8,128)(2,1)} %reshape.591), calls=%async_computation.1 | async-start | bytes 4194304 | tf_op jit(solution)/shard_map/all_to_all | solution.py:82
  115.8 0.2 all-gather.5.cloned.1.call-start
  116.1 0.7 fusion.44
  116.8 1.0 convolution_multiply_fusion
  117.8 1.2 copy.144
  119.9 0.2 fusion.19
  120.1 0.7 copy.121
  120.8 1.5 fusion.23
  122.3 1.5 copy.130
  123.8 1.1 convolution_bitcast_fusion.1
  124.9 0.8 copy.125
  125.7 1.0 reshape.537
  126.8 0.8 reshape.595
  127.6 0.6 copy-done.8
  128.2 0.6 reduce_max.44
  128.8 0.7 reshape.597
  129.6 1.5 subtract_exponential_fusion
  131.1 1.8 copy.112
  132.9 3.3 %mul.94 = f32[16,28,16,128]{3,2,0,1:T(8,128)} broadcast(f32[16,28,16]{2,0,1:T(8,128)} %copy.112), dimensions={0,1,2} | broadcast | bytes 3698688 | tf_op jit(solution)/shard_map/mul | solution.py:90
  136.2 4.8 %mul.95 = f32[16,28,2048]{2,0,1:T(8,128)} reshape(f32[16,28,16,128]{3,2,0,1:T(8,128)} %mul.94) | data formatting | bytes 7340032 | tf_op jit(solution)/shard_map/mul | solution.py:90
  141.0 0.8 div.18
  141.9 1.7 div.19
  143.6 0.8 mul.100
  144.4 1.7 mul.101
  146.2 0.8 mul.103
  147.0 1.7 mul.104
  148.7 8.4 %all-to-all-done.1 = bf16[16,28,2048]{2,1,0:T(8,128)(2,1)S(1)} async-done(((bf16[16,28,2048]{2,1,0:T(8,128)(2,1)}), bf16[16,28,2048]{2,1,0:T(8,128)(2,1)S(1)}, u32[]{:S(2)}, u32[]{:S(2)}) %all-to-all-start.1) | async-done | bytes 1835040 | tf_op jit(solution)/shard_map/all_to_all | solution.py:82
  157.1 3.7 %multiply_reduce_fusion = f32[28,2048]{1,0:T(8,128)S(1)} fusion(f32[16,28,2048]{2,0,1:T(8,128)} %mul.95, bf16[16,28,2048]{2,1,0:T(8,128)(2,1)S(1)} %all-to-all-done.1), kind=kLoop, calls=%fused_computation.6 | loop fusion | flops 2695168 | bytes 5734400 | tf_op jit(solution)/shard_map/reduce_sum | solution.py:90
  160.8 0.7 fusion.18
  161.9 0.6 gather_fusion.3
  162.7 45.7 %all_gather.11 = bf16[16,8,1024]{2,1,0:T(8,128)(2,1)S(1)} all-gather(bf16[1,8,1024]{2,1,0:T(8,128)(2,1)S(1)} %bitcast_select_fusion.1), channel_id=1, replica_groups=mesh['req'=16,'tp'=2] {'req'}, dimensions={0}, use_global_device_ids=true | all-gather | bytes 278528 | tf_op jit(solution)/shard_map/all_gather | solution.py:127
  208.4 0.7 gather_fusion.4
  209.1 18.0 %all-gather.5.cloned.1.call-done = bf16[16,28,2048]{2,1,0:T(8,128)(2,1)} async-done(((bf16[1,28,2048]{2,1,0:T(8,128)(2,1)}), bf16[16,28,2048]{2,1,0:T(8,128)(2,1)}) %all-gather.5.cloned.1.call-update) | async-done | bytes 1835024 | tf_op jit(solution)/shard_map/all_gather | solution.py:119
  227.1 3.0 %convolution_convert_fusion = bf16[16,28,256]{2,1,0:T(8,128)(2,1)} fusion(bf16[16,28,2048]{2,1,0:T(8,128)(2,1)} %all-gather.5.cloned.1.call-done, bf16[2048,256]{1,0:T(8,128)(2,1)S(1)} %copy-done), kind=kOutput, calls=%fused_computation.17 | convolution fusion | flops 469876736 | bytes 3112960 | tf_op jit(solution)/shard_map/dot_general | solution.py:121
  230.2 7.3 %gather_fusion.5 = bf16[768,1024]{1,0:T(8,128)(2,1)S(1)} fusion(bf16[3,8,1024]{2,1,0:T(8,128)(2,1)S(1)} %gather_fusion.4, s32[768]{0:T(1024)S(1)} %reshape.579), kind=kCustom, calls=%fused_computation.5 | custom fusion | bytes 3151872 | tf_op jit(solution)/shard_map/jit(take_along_axis)/gather | solution.py:132
  237.6 2.9 %select_select_fusion = bf16[3,256,1024]{2,1,0:T(8,128)(2,1)} fusion(bf16[3,256,1024]{2,1,0:T(8,128)(2,1)} %param.12, bf16[3,256,1024]{2,1,0:T(8,128)(2,1)S(1)} %bitcast.114, pred[3,256]{1,0:T(4,128)(4,1)S(1)} %copy-done.18, pred[3,256]{1,0:T(4,128)(4,1)S(1)} %copy-done.17), kind=kLoop, calls=%fused_computation.12 | loop fusion | flops 1572864 | bytes 4720128 | tf_op jit(solution)/shard_map/jit(_where)/select_n | solution.py:133
  240.5 1.6 copy.132
  (71 shorter events, 2.3 us)
Async XLA Ops:
  7.2 219.9 %copy-start = (bf16[2048,256]{1,0:T(8,128)(2,1)S(1)}, bf16[2048,256]{1,0:T(8,128)(2,1)}, u32[]{:S(2)}) copy-start(bf16[2048,256]{1,0:T(8,128)(2,1)} %param.15) | copy-start | bytes 3145732
  7.2 67.0 %all-gather.3.cloned.1.call-start = ((), (), s32[]{:S(2)}) async-start(), calls=%async_computation.4 | async-start | bytes 2228224 | tf_op jit(solution)/shard_map/all_gather | solution.py:37
  8.7 5.3 %copy-start.13 = (s32[3]{0:T(128)}, s32[3]{0:T(128)S(1)}, u32[]{:S(2)}) copy-start(s32[3]{0:T(128)S(1)} %get-tuple-element.28) | copy-start | bytes 40
  8.7 65.5 %copy-start.12 = (s32[1024]{0:T(1024)}, s32[1024]{0:T(1024)S(1)}, u32[]{:S(2)}) copy-start(s32[1024]{0:T(1024)S(1)} %pad_clamp_fusion.1) | copy-start | bytes 12292
  10.0 4.0 %copy-start.15 = (s32[3]{0:T(128)}, s32[3]{0:T(128)S(1)}, u32[]{:S(2)}) copy-start(s32[3]{0:T(128)S(1)} %gather_fusion) | copy-start | bytes 40
  11.3 2.7 %copy-start.19 = (s32[3,2]{0,1:T(2,128)S(1)}, s32[3,2]{0,1:T(2,128)}, u32[]{:S(2)}) copy-start(s32[3,2]{0,1:T(2,128)} %param.13) | copy-start | bytes 76
  82.2 11.6 %all-to-all-start.2 = ((bf16[16,2,224]{2,1,0:T(2,128)(2,1)}), bf16[16,2,224]{2,1,0:T(2,128)(2,1)S(1)}, u32[]{:S(2)}, u32[]{:S(2)}) async-start(bf16[16,2,224]{2,1,0:T(2,128)(2,1)} %reshape.596), calls=%async_computation.2 | async-start | bytes 32768 | tf_op jit(solution)/shard_map/all_to_all | solution.py:79
  93.8 14.4 %all-to-all-start = ((bf16[16,2,224]{2,1,0:T(2,128)(2,1)}), bf16[16,2,224]{2,1,0:T(2,128)(2,1)S(1)}, u32[]{:S(2)}, u32[]{:S(2)}) async-start(bf16[16,2,224]{2,1,0:T(2,128)(2,1)} %reshape.594), calls=%async_computation | async-start | bytes 32768 | tf_op jit(solution)/shard_map/all_to_all | solution.py:76
  108.3 7.7 %copy-start.5 = (bf16[1,28,2048]{2,1,0:T(8,128)(2,1)S(1)}, bf16[1,28,2048]{2,1,0:T(8,128)(2,1)}, u32[]{:S(2)}) copy-start(bf16[1,28,2048]{2,1,0:T(8,128)(2,1)} %param.8) | copy-start | bytes 344068
  108.3 7.8 %copy-start.4 = (bf16[1,28,1024]{2,1,0:T(8,128)(2,1)S(1)}, bf16[1,28,1024]{2,1,0:T(8,128)(2,1)}, u32[]{:S(2)}) copy-start(bf16[1,28,1024]{2,1,0:T(8,128)(2,1)} %param.9) | copy-start | bytes 172036
  108.3 10.7 %copy-start.20 = (s32[1,28]{1,0:T(1,128)S(1)}, s32[1,28]{1,0:T(1,128)}, u32[]{:S(2)}) copy-start(s32[1,28]{1,0:T(1,128)} %param.10) | copy-start | bytes 340
  108.3 0.6 copy-start.6
  108.9 48.2 %all-to-all-start.1 = ((bf16[16,28,2048]{2,1,0:T(8,128)(2,1)}), bf16[16,28,2048]{2,1,0:T(8,128)(2,1)S(1)}, u32[]{:S(2)}, u32[]{:S(2)}) async-start(bf16[16,28,2048]{2,1,0:T(8,128)(2,1)} %reshape.591), calls=%async_computation.1 | async-start | bytes 4194304 | tf_op jit(solution)/shard_map/all_to_all | solution.py:82
  115.8 111.3 %all-gather.5.cloned.1.call-start = ((), (), s32[]{:S(2)}) async-start(), calls=%async_computation.5 | async-start | bytes 2228224 | tf_op jit(solution)/shard_map/all_gather | solution.py:119
  127.6 0.6 copy-start.8
  136.2 4.8 %copy-start.9 = (bf16[28,16]{0,1:T(8,128)(2,1)S(1)}, bf16[28,16]{0,1:T(8,128)(2,1)}, u32[]{:S(2)}) copy-start(bf16[28,16]{0,1:T(8,128)(2,1)} %copy-done.8) | copy-start | bytes 2692
  136.2 4.8 %copy-start.10 = (f32[28,4,4]{0,2,1:T(4,128)S(1)}, f32[28,4,4]{0,2,1:T(4,128)}, u32[]{:S(2)}) copy-start(f32[28,4,4]{0,2,1:T(4,128)} %copy.121) | copy-start | bytes 5380
  136.2 4.8 %copy-start.11 = (f32[28,4,4]{0,2,1:T(4,128)S(1)}, f32[28,4,4]{0,2,1:T(4,128)}, u32[]{:S(2)}) copy-start(f32[28,4,4]{0,2,1:T(4,128)} %copy.130) | copy-start | bytes 5380
  157.0 3.8 %copy-start.1 = (f32[1,28,2048]{2,1,0:T(8,128)S(1)}, f32[1,28,2048]{2,1,0:T(8,128)}, u32[]{:S(2)}) copy-start(f32[1,28,2048]{2,1,0:T(8,128)} %div.19) | copy-start | bytes 688132
  157.0 3.8 %copy-start.2 = (f32[1,28,2048]{2,1,0:T(8,128)S(1)}, f32[1,28,2048]{2,1,0:T(8,128)}, u32[]{:S(2)}) copy-start(f32[1,28,2048]{2,1,0:T(8,128)} %mul.101) | copy-start | bytes 688132
  157.1 3.8 %copy-start.3 = (f32[1,28,2048]{2,1,0:T(8,128)S(1)}, f32[1,28,2048]{2,1,0:T(8,128)}, u32[]{:S(2)}) copy-start(f32[1,28,2048]{2,1,0:T(8,128)} %mul.104) | copy-start | bytes 688132
  160.8 0.8 copy-start.7
  161.6 78.9 %reduce-scatter.2.cloned.1.call-start = ((), (), s32[]{:S(2)}) async-start(), calls=%async_computation.6 | async-start | bytes 393216 | tf_op jit(solution)/shard_map/reduce_scatter | solution.py:123
  209.0 21.1 %copy-start.14 = (s32[3]{0:T(128)S(1)}, s32[3]{0:T(128)}, u32[]{:S(2)}) copy-start(s32[3]{0:T(128)} %copy-done.13) | copy-start | bytes 40
  209.0 21.1 %copy-start.16 = (s32[3]{0:T(128)S(1)}, s32[3]{0:T(128)}, u32[]{:S(2)}) copy-start(s32[3]{0:T(128)} %copy-done.15) | copy-start | bytes 40
  230.2 7.4 %copy-start.17 = (pred[3,256]{1,0:T(4,128)(4,1)S(1)}, pred[3,256]{1,0:T(4,128)(4,1)}, u32[]{:S(2)}) copy-start(pred[3,256]{1,0:T(4,128)(4,1)} %get-tuple-element.23) | copy-start | bytes 2308
  230.2 7.4 %copy-start.18 = (pred[3,256]{1,0:T(4,128)(4,1)S(1)}, pred[3,256]{1,0:T(4,128)(4,1)}, u32[]{:S(2)}) copy-start(pred[3,256]{1,0:T(4,128)(4,1)} %get-tuple-element.25) | copy-start | bytes 2308
Sparse Core Ops, SparseCore 0:
  10.8 63.3 all-gather.2
  161.7 65.3 all-gather.4
  230.2 6.2 reduce-scatter.1
where the time goes:
time: 250 us; the launch traced here: 249 us
  waiting for transfers between devices  90.5 us (36%)
  local copies, waits for them, and re-layouts  48.9 us (20%)
  blocking collectives  45.7 us (18%)
  matrix products  17.8 us (7%)
  other arithmetic  16.7 us (7%)
  starting transfers between devices  14.9 us (6%)
  between operations  14.1 us (6%)
    all_gather x1, waiting for transfers between devices, shards(): every_query = lax.all_gather(queries, 'req', axis=0, tiled=True)  59.5 us
    all_gather x1, blocking collectives, shards(): all_rows = lax.all_gather(picked[None], 'req', axis=0, tiled=True)  45.7 us
    all_gather x1, waiting for transfers between devices, shards(): piece = lax.all_gather(attention, 'req', axis=0, tiled=True)  18 us
    unnamed x49, local copies, waits for them, and re-layouts  9.66 us
    all_to_all x1, waiting for transfers between devices, shards(): lax.all_to_all(num_table.astype(jnp.bfloat16), 'req', split_axis=0, conca...  8.37 us
    mul x2, local copies, waits for them, and re-layouts, shards(): cache_num = jnp.sum(source_scale[..., None] * got_rows, axis=0)  8.04 us
    dot_general x1, matrix products, shards(): jnp.einsum('rstkg,stkgd->rtkgd', factor, slot_num, precision=lax.Precisio...  7.9 us
    gather x2, local copies, waits for them, and re-layouts, shards(): jnp.take_along_axis(slot_rows, jnp.clip(offset, 0, depth_most - 1)[:, :,...  7.36 us
  transfers between devices with their start and end apart: 6, of which 4 were waited for; matrix products, arithmetic and copies ran while one was open for 26% of the time, Pallas kernels for 0%

commit v1 on v0

--- a/solution.py
+++ b/solution.py
@@ -3,6 +3,8 @@
 import jax
 import jax.numpy as jnp
 from jax import lax
+from jax.experimental import pallas as pl
+from jax.experimental.pallas import tpu as pltpu
 from jax.sharding import PartitionSpec as P
 
 HD = 128
@@ -23,7 +25,7 @@
     return reached
 
 
-def shards(
+def shards_general(
     queries, tree_kv, tree_parent, accepted_path, cache_kv, piece_owner, cache_len, out_weight
 ):
     kvheads_local = tree_kv.shape[-1] // (2 * HD)
@@ -134,9 +136,404 @@
     return (mixed, cache_out)
 
 
+MESH = pl.DeviceIdType.MESH
+PAD = 32
+KINDS = 19
+
+
+def place():
+    me = lax.axis_index("req")
+    z, y, x = me // 4, (me // 2) % 2, me % 2
+    planes = [z, z + 1 - 2 * (z % 2), (z + 2) % 4, 3 - z]
+    return me, y, x, planes
+
+
+class GridGather:
+    def __init__(self, buf, send, recv):
+        me, y, x, planes = place()
+        self.buf, self.send, self.recv = buf, send, recv
+        self.column = [plane * 4 + y * 2 + x for plane in planes]
+        self.to_x, self.to_y = 1 - 2 * x, 2 - 4 * y
+        self.me = me
+        self.sent = []
+
+    def copy(self, origin, part, target, kind):
+        rows = self.buf.shape[1]
+        half = rows // 2
+        start, size = {"all": (0, rows), "top": (0, half), "low": (half, half)}[part]
+        block = self.buf.at[origin, pl.ds(start, size)]
+        return pltpu.make_async_remote_copy(
+            src_ref=block,
+            dst_ref=block,
+            send_sem=self.send.at[kind],
+            recv_sem=self.recv.at[kind],
+            device_id={"req": target},
+            device_id_type=MESH,
+        )
+
+    def go(self, *args):
+        moving = self.copy(*args)
+        moving.start()
+        self.sent.append(moving)
+
+    def run(self):
+        me, column = self.me, self.column
+        near_x, near_y = me + self.to_x, me + self.to_y
+        for k in range(1, 4):
+            self.go(me, "all", column[k], k - 1)
+        for k in range(5):
+            if k < 4:
+                if k:
+                    self.copy(column[k], "all", near_x, k - 1).wait_recv()
+                self.go(column[k], "all", near_x, 3 + k)
+                self.go(column[k], "all", near_y, 7 + k)
+            if k:
+                before = column[k - 1]
+                self.copy(before + self.to_x, "all", near_x, 2 + k).wait_recv()
+                self.go(before + self.to_x, "top", near_y, 10 + k)
+                self.copy(before + self.to_y, "all", near_x, 6 + k).wait_recv()
+                self.go(before + self.to_y, "low", near_x, 14 + k)
+        for k in range(4):
+            across = column[k] + self.to_x + self.to_y
+            self.copy(across, "top", near_x, 11 + k).wait_recv()
+            self.copy(across, "low", near_x, 15 + k).wait_recv()
+
+    def finish(self):
+        for moving in self.sent:
+            moving.wait_send()
+
+
+def iota(shape, dim):
+    return lax.broadcasted_iota(jnp.int32, shape, dim)
+
+
+def as_column(row):
+    size = row.shape[1]
+    shape = (size, size)
+    return jnp.sum(
+        jnp.where(iota(shape, 0) == iota(shape, 1), row, 0.0), axis=1, keepdims=True
+    )
+
+
+def attend(query, key, value, mask, scaling, owner):
+    rows = query.shape[0]
+    scores = scaling * lax.dot_general(
+        query, key, (((1,), (1,)), ((), ())), preferred_element_type=jnp.float32
+    )
+    scores = jnp.where(mask, scores, NEG)
+    peak = jnp.max(scores, axis=1, keepdims=True)
+    expo = jnp.where(mask, jnp.exp(scores - peak), 0.0)
+    denom = jnp.sum(expo, axis=1, keepdims=True)
+    numer = jnp.dot(expo.astype(jnp.bfloat16), value, preferred_element_type=jnp.float32)
+    some = denom > 0.0
+    safe = jnp.where(some, denom, 1.0)
+    level = jnp.where(some, peak + jnp.log(safe), NEG)
+    out = numer * (1.0 / safe)
+    shape = (PAD, HD)
+    pick = iota(shape, 0) == iota(shape, 1)
+    where = iota(shape, 0)
+    blocks = []
+    for g in range(rows // PAD):
+        line = jnp.sum(
+            jnp.where(pick, level[g * PAD : (g + 1) * PAD], 0.0), axis=0, keepdims=True
+        )
+        high = line.astype(jnp.bfloat16).astype(jnp.float32)
+        block = out[g * PAD : (g + 1) * PAD]
+        block = jnp.where(where == 28, high, block)
+        block = jnp.where(where == 29, line - high, block)
+        block = jnp.where(where == 30, owner, block)
+        blocks.append(block.astype(jnp.bfloat16))
+    return blocks
+
+
+def layer_kernel(
+    owner_ref, len_ref, parent_ref, path_ref, query_ref, tree_ref, cache_ref, weight_ref,
+    mixed_ref, rows_ref,
+    cache_v, weight_v, gathered, packed, tree_f, tree_b, reach_v, outgoing, incoming,
+    wide, owners, joined, compact, attn, half_out, half_in,
+    local_sem, send1, recv1, send2, recv2, send3, recv3, send4, recv4,
+):
+    me, y, x, planes = place()
+    tp = lax.axis_index("tp")
+    tree_size = query_ref.shape[1]
+    slots = cache_ref.shape[0]
+    piece_rows = cache_ref.shape[1]
+    scaling = 1.0 / math.sqrt(HD)
+    load_cache = pltpu.make_async_copy(cache_ref, cache_v, local_sem.at[0])
+    load_weight = pltpu.make_async_copy(weight_ref, weight_v, local_sem.at[1])
+    load_cache.start()
+    load_weight.start()
+
+    barrier = pltpu.get_barrier_semaphore()
+    for d in range(1, 16):
+        pl.semaphore_signal(
+            barrier, inc=1, device_id={"req": (me + d) % 16}, device_id_type=MESH
+        )
+    pl.semaphore_signal(barrier, inc=1, device_id={"tp": 1 - tp}, device_id_type=MESH)
+
+    tree_f[...] = jnp.zeros_like(tree_f)
+    tree_f[0:tree_size] = tree_ref[0].astype(jnp.float32)
+    tree_b[...] = tree_f[...].astype(jnp.bfloat16)
+    path = as_column(path_ref[pl.ds(me, 1), :].astype(jnp.float32))
+    depth = path.shape[0]
+    chosen = (path == iota((depth, PAD), 1).astype(jnp.float32)).astype(jnp.bfloat16)
+    picked = jnp.dot(chosen, tree_b[...], preferred_element_type=jnp.float32)
+    width = tree_ref.shape[2]
+    packed[0:tree_size] = query_ref[0].astype(jnp.float32)
+    packed[tree_size:PAD, 0:width] = picked[0:4]
+    packed[tree_size:PAD, width : 2 * width] = picked[4:8]
+    gathered[me] = packed[...].astype(jnp.bfloat16)
+
+    pl.semaphore_wait(barrier, 16)
+    first = GridGather(gathered, send1, recv1)
+    first.run()
+
+    parent = as_column(parent_ref[...].astype(jnp.float32))
+    lanes = iota((tree_size, PAD), 1).astype(jnp.float32)
+    reach_v[...] = (iota((PAD, PAD), 0) == iota((PAD, PAD), 1)).astype(jnp.float32)
+    reach_v[0:tree_size] = jnp.minimum(
+        reach_v[0:tree_size] + (parent == lanes).astype(jnp.float32), 1.0
+    )
+    reached = reach_v[...]
+    for rounds in range(max(1, (tree_size - 1).bit_length())):
+        short = reached.astype(jnp.bfloat16)
+        reached = jnp.minimum(jnp.dot(short, short, preferred_element_type=jnp.float32), 1.0)
+    tree_mask = jnp.concatenate([reached] * 4, axis=0) > 0.5
+
+    load_cache.wait()
+    sent = []
+    for k in range(4):
+        plane = planes[k]
+        for s in range(slots + 1):
+            if s < slots:
+                owner = owner_ref[s, 0]
+                request = jnp.maximum(owner, 0)
+                limit = jnp.where(owner >= 0, len_ref[request] - owner_ref[s, 1] * piece_rows, 0)
+                mask = iota((4 * PAD, piece_rows), 1) < limit
+                source, keys = request, cache_v.at[s]
+                if k == 0:
+                    rows_ref[s] = gathered[request, 16:32, :]
+            else:
+                owner, source, keys, mask = me, me, tree_b, tree_mask
+            start = pl.multiple_of(plane * 4 * HD, 4 * HD)
+            wide_q = gathered[source, :, pl.ds(start, 4 * HD)]
+            query = jnp.concatenate([wide_q[:, g * HD : (g + 1) * HD] for g in range(4)], axis=0)
+            at = pl.multiple_of(plane * 2 * HD, 2 * HD)
+            both = keys[:, pl.ds(at, 2 * HD)]
+            blocks = attend(
+                query, both[:, :HD], both[:, HD:], mask, scaling, owner.astype(jnp.float32)
+            )
+            for g in range(4):
+                outgoing[4 * k + g, s * PAD : (s + 1) * PAD] = blocks[g]
+        for g in range(4):
+            target = plane * 4 + g
+
+            def remote(target=target, n=4 * k + g):
+                return pltpu.make_async_remote_copy(
+                    src_ref=outgoing.at[n],
+                    dst_ref=incoming.at[me],
+                    send_sem=send2.at[n],
+                    recv_sem=recv2.at[me],
+                    device_id={"req": target},
+                    device_id_type=MESH,
+                )
+
+            if k == 0:
+
+                @pl.when(target != me)
+                def _():
+                    remote().start()
+
+                @pl.when(target == me)
+                def _():
+                    incoming[me] = outgoing[g]
+
+            else:
+                remote().start()
+            sent.append((k, target, remote))
+    for d in range(1, 16):
+        source = (me + d) % 16
+        pltpu.make_async_remote_copy(
+            src_ref=outgoing.at[0],
+            dst_ref=incoming.at[source],
+            send_sem=send2.at[0],
+            recv_sem=recv2.at[source],
+            device_id={"req": source},
+            device_id_type=MESH,
+        ).wait_recv()
+
+    pieces = 16 * (slots + 1)
+    wide[...] = incoming[...].astype(jnp.float32).reshape(pieces * PAD, HD)
+    level = wide[pl.ds(28, pieces, stride=PAD), :] + wide[pl.ds(29, pieces, stride=PAD), :]
+    holder = wide[pl.ds(30, pieces, stride=PAD), :]
+    owners[...] = holder
+    share = jnp.zeros_like(level)
+    for r in range(16):
+        member = holder == float(r)
+        peak = jnp.max(jnp.where(member, level, NEG), axis=0, keepdims=True)
+        expo = jnp.where(member, jnp.exp(jnp.where(member, level - peak, 0.0)), 0.0)
+        share = share + expo * (1.0 / jnp.sum(expo, axis=0, keepdims=True))
+    turned = share.T
+    for b in range(pieces):
+        block = slice(b * PAD, (b + 1) * PAD)
+        wide[block] = wide[block] * turned[0:PAD, b : b + 1]
+
+    def join(r, carry):
+        mine = r.astype(jnp.float32)
+        first_row = pl.multiple_of((r * (slots + 1) + slots) * PAD, PAD)
+        total = wide[pl.ds(first_row, PAD), :]
+        for b in range(pieces):
+            if b % (slots + 1) < slots:
+                total = total + jnp.where(
+                    owners[b : b + 1] == mine, wide[b * PAD : (b + 1) * PAD], 0.0
+                )
+        joined[r] = total
+        return carry
+
+    lax.fori_loop(0, 16, join, 0)
+    for r in range(16):
+        compact[r * tree_size : (r + 1) * tree_size] = joined[r, 0:tree_size]
+    attn[me] = compact[...].astype(jnp.bfloat16)
+
+    last = GridGather(attn, send3, recv3)
+    last.run()
+    load_weight.wait()
+    size = half_out.shape[0]
+
+    def project(part):
+        begin = pl.multiple_of(part * size, size)
+        total = jnp.zeros(half_out.shape, jnp.float32)
+        for j in range(0, 16, 2):
+            pair = jnp.concatenate(
+                [attn[j, pl.ds(begin, size), :], attn[j + 1, pl.ds(begin, size), :]], axis=1
+            )
+            total = total + jnp.dot(
+                pair, weight_v[j * HD : (j + 2) * HD], preferred_element_type=jnp.float32
+            )
+        return total
+
+    half_out[...] = project(1 - tp).astype(jnp.bfloat16)
+    swap = pltpu.make_async_remote_copy(
+        src_ref=half_out,
+        dst_ref=half_in,
+        send_sem=send4,
+        recv_sem=recv4,
+        device_id={"tp": 1 - tp},
+        device_id_type=MESH,
+    )
+    swap.start()
+    own_half = project(tp)
+    swap.wait_recv()
+    mixed_ref[...] = (own_half + half_in[...].astype(jnp.float32)).astype(jnp.bfloat16)
+
+    swap.wait_send()
+    first.finish()
+    last.finish()
+    for k, target, remote in sent:
+        if k == 0:
+
+            @pl.when(target != me)
+            def _():
+                remote().wait_send()
+
+        else:
+            remote().wait_send()
+
+
+def append_kernel(owner_ref, len_ref, path_ref, cache_ref, rows_ref, out_ref):
+    s = pl.program_id(0)
+    owner = owner_ref[s, 0]
+    request = jnp.maximum(owner, 0)
+    piece_rows, width = cache_ref.shape[1], cache_ref.shape[2]
+    count = jnp.int32(0)
+    for j in range(path_ref.shape[1]):
+        count = count + (path_ref[request, j] >= 0).astype(jnp.int32)
+    count = jnp.where(owner >= 0, count, 0)
+    begin = len_ref[request] - owner_ref[s, 1] * piece_rows
+    offset = iota((piece_rows, 16), 0) - begin
+    lane = iota((piece_rows, 16), 1) - 12
+    low = ((offset == lane) & (lane >= 0)).astype(jnp.bfloat16)
+    high = ((offset == lane + 4) & (lane >= 0)).astype(jnp.bfloat16)
+    rows = rows_ref[0]
+    chosen = jnp.dot(low, rows[:, :width], preferred_element_type=jnp.float32) + jnp.dot(
+        high, rows[:, width:], preferred_element_type=jnp.float32
+    )
+    offset = iota((piece_rows, width), 0) - begin
+    writing = (offset >= 0) & (offset < count)
+    out_ref[0] = jnp.where(writing, chosen, cache_ref[0].astype(jnp.float32)).astype(jnp.bfloat16)
+
+
+def shards_grid(
+    queries, tree_kv, tree_parent, accepted_path, cache_kv, piece_owner, cache_len, out_weight
+):
+    slots, piece_rows, width = cache_kv.shape
+    tree_size = queries.shape[1]
+    columns = queries.shape[2]
+    reqs = 16
+    half = reqs * tree_size // 2
+    smem = pl.BlockSpec(memory_space=pltpu.SMEM)
+    vmem = pl.BlockSpec(memory_space=pltpu.VMEM)
+    anywhere = pl.BlockSpec(memory_space=pl.ANY)
+    pieces = reqs * (slots + 1)
+    dma = pltpu.SemaphoreType.DMA
+    bf16, f32 = jnp.bfloat16, jnp.float32
+    mixed, rows = pl.pallas_call(
+        layer_kernel,
+        out_shape=(
+            jax.ShapeDtypeStruct((half, out_weight.shape[1]), bf16),
+            jax.ShapeDtypeStruct((slots, 16, columns), bf16),
+        ),
+        in_specs=[smem, smem, vmem, vmem, vmem, vmem, anywhere, anywhere],
+        out_specs=(vmem, vmem),
+        scratch_shapes=[
+            pltpu.VMEM(cache_kv.shape, bf16),
+            pltpu.VMEM(out_weight.shape, bf16),
+            pltpu.VMEM((reqs, PAD, columns), bf16),
+            pltpu.VMEM((PAD, columns), f32),
+            pltpu.VMEM((PAD, width), f32),
+            pltpu.VMEM((PAD, width), bf16),
+            pltpu.VMEM((PAD, PAD), f32),
+            pltpu.VMEM((reqs, (slots + 1) * PAD, HD), bf16),
+            pltpu.VMEM((reqs, (slots + 1) * PAD, HD), bf16),
+            pltpu.VMEM((pieces * PAD, HD), f32),
+            pltpu.VMEM((pieces, HD), f32),
+            pltpu.VMEM((reqs, PAD, HD), f32),
+            pltpu.VMEM((reqs * tree_size, HD), f32),
+            pltpu.VMEM((reqs, reqs * tree_size, HD), bf16),
+            pltpu.VMEM((half, out_weight.shape[1]), bf16),
+            pltpu.VMEM((half, out_weight.shape[1]), bf16),
+            dma((2,)),
+            dma((KINDS,)),
+            dma((KINDS,)),
+            dma((reqs,)),
+            dma((reqs,)),
+            dma((KINDS,)),
+            dma((KINDS,)),
+            dma,
+            dma,
+        ],
+        compiler_params=pltpu.CompilerParams(
+            collective_id=0, has_side_effects=True, vmem_limit_bytes=48 * 1024 * 1024
+        ),
+    )(
+        piece_owner, cache_len, tree_parent, accepted_path, queries, tree_kv, cache_kv, out_weight
+    )
+    block = pl.BlockSpec((1, piece_rows, width), lambda s: (s, 0, 0))
+    cache_out = pl.pallas_call(
+        append_kernel,
+        out_shape=jax.ShapeDtypeStruct(cache_kv.shape, bf16),
+        grid=(slots,),
+        in_specs=[smem, smem, smem, block, pl.BlockSpec((1, 16, columns), lambda s: (s, 0, 0))],
+        out_specs=block,
+        compiler_params=pltpu.CompilerParams(vmem_limit_bytes=32 * 1024 * 1024),
+    )(piece_owner, cache_len, accepted_path, cache_kv, rows)
+    return mixed.reshape(reqs // 2, tree_size, out_weight.shape[1]), cache_out
+
+
 def solution(mesh):
+    body = shards_grid if dict(mesh.shape) == {"req": 16, "tp": 2} else shards_general
     return jax.shard_map(
-        shards,
+        body,
         mesh=mesh,
         in_specs=(
             P("req", None, "tp"),

time: 250 us -> 77.5 us (0.31)
  waiting for transfers between devices: 90.5 us -> 0 us
  Pallas kernels: 0 us -> 68.6 us
  blocking collectives: 45.7 us -> 0 us
  local copies, waits for them, and re-layouts: 48.9 us -> 7.95 us
  matrix products: 17.8 us -> 0 us
  other arithmetic: 16.7 us -> 0 us
  starting transfers between devices: 14.9 us -> 0 us
  between operations: 14.1 us -> 0.66 us
    all_gather x2 -> x0, waiting for transfers between devices: 77.5 us -> none  [the longest x1 59.5 us: shards(): every_query = lax.all_gather(queries, 'req', axis=0, tiled=True)]
    pallas_call x0 -> x2, Pallas kernels: none -> 68.6 us  [the longest x1 65.5 us: shards_grid(): pl.pallas_call(layer_kernel, out_shape=(jax.ShapeDtypeStruct((half, out_w...]
    all_gather x1 -> x0, blocking collectives: 45.7 us -> none  [shards(): all_rows = lax.all_gather(picked[None], 'req', axis=0, tiled=True)]
    dot_general x11 -> x0, matrix products: 17.8 us -> none  [the longest x1 7.9 us: shards(): jnp.einsum('rstkg,stkgd->rtkgd', factor, slot_num, precision=lax.Precisio...]
    all_to_all x3 -> x0, starting transfers between devices: 14.6 us -> none  [the longest x1 6.87 us: shards(): lax.all_to_all(num_table.astype(jnp.bfloat16), 'req', split_axis=0, conca...]
    mul x6 -> x0, local copies, waits for them, and re-layouts: 13 us -> none  [the longest x2 8.04 us: shards(): cache_num = jnp.sum(source_scale[..., None] * got_rows, axis=0)]
    gather x7 -> x0, local copies, waits for them, and re-layouts: 12.7 us -> none  [the longest x2 7.36 us: shards(): jnp.take_along_axis(slot_rows, jnp.clip(offset, 0, depth_most - 1)[:, :,...]
    all_to_all x3 -> x0, waiting for transfers between devices: 12.3 us -> none  [the longest x1 8.37 us: shards(): lax.all_to_all(num_table.astype(jnp.bfloat16), 'req', split_axis=0, conca...]
  transfers between devices with their start and end apart: 6 -> 0, of which waited for: 4 -> 0; matrix products, arithmetic and copies ran while one was open for 26% -> 0% of each run, Pallas kernels for 0% -> 0%
where the time goes in v1:
time: 77.5 us; the launch traced here: 77.2 us
  Pallas kernels  68.6 us (89%)
  local copies, waits for them, and re-layouts  7.95 us (10%)
    pallas_call x1, Pallas kernels, shards_grid(): pl.pallas_call(layer_kernel, out_shape=(jax.ShapeDtypeStruct((half, out_w...  65.5 us
    unnamed x19, local copies, waits for them, and re-layouts  7.93 us
    pallas_call x1, Pallas kernels, shards_grid(): pl.pallas_call(append_kernel, out_shape=jax.ShapeDtypeStruct(cache_kv.sha...  3.14 us

profile of v1, /device:TPU:0, one launch (start us, length us, event | category | flops | bytes accessed | tf_op | source)
XLA Modules:
  0.0 77.2 jit_solution(2944937568428838227)
XLA Ops:
  0.6 0.8 copy.15.owner_ref
  1.4 0.8 copy.16.path_ref
  2.2 0.0 copy-start
  2.2 1.4 %copy-done = bf16[3,256,1024]{2,1,0:T(8,128)(2,1)S(1)} copy-done((bf16[3,256,1024]{2,1,0:T(8,128)(2,1)S(1)}, bf16[3,256,1024]{2,1,0:T(8,128)(2,1)}, u32[]{:S(2)}) %copy-start) | copy-done | bytes 1572888
  3.6 0.0 copy-start.2
  3.6 1.2 %copy-done.2 = bf16[2048,256]{1,0:T(8,128)(2,1)S(1)} copy-done((bf16[2048,256]{1,0:T(8,128)(2,1)S(1)}, bf16[2048,256]{1,0:T(8,128)(2,1)}, u32[]{:S(2)}) %copy-start.2) | copy-done | bytes 1048600
  4.8 0.0 copy-start.3
  4.8 0.9 %copy-done.3 = bf16[1,28,2048]{2,1,0:T(8,128)(2,1)S(1)} copy-done((bf16[1,28,2048]{2,1,0:T(8,128)(2,1)S(1)}, bf16[1,28,2048]{2,1,0:T(8,128)(2,1)}, u32[]{:S(2)}) %copy-start.3) | copy-done | bytes 114712
  5.7 0.0 copy-start.4
  5.7 0.8 %copy-done.4 = bf16[1,28,1024]{2,1,0:T(8,128)(2,1)S(1)} copy-done((bf16[1,28,1024]{2,1,0:T(8,128)(2,1)S(1)}, bf16[1,28,1024]{2,1,0:T(8,128)(2,1)}, u32[]{:S(2)}) %copy-start.4) | copy-done | bytes 57368
  6.5 0.0 copy-start.5
  6.5 0.7 copy-done.5
  7.2 0.0 copy-start.7
  7.2 0.7 copy-done.7
  7.8 0.0 copy-start.1
  7.8 0.0 copy-start.6
  7.8 65.5 %shard_map.95 = (bf16[224,256]{1,0:T(8,128)(2,1)S(1)}, bf16[3,16,2048]{2,1,0:T(8,128)(2,1)S(1)}) custom-call(s32[3,2]{1,0:T(4,128)S(1)} %copy.15.owner_ref, s32[16]{0:T(128)S(1)} %copy-done.5, s32[1,28]{1,0:T(1,128)S(1)} %copy-done.7, s32[16,8]{1,0:T(8,128)S(1)} %copy.16.path_ref, bf16[1,28,2048]{2,1,0:T(8,128)(2,1)S(1)} %copy-done.3, ...), custom_call_target="tpu_custom_call" | custom-call | tf_op jit(solution)/shard_map/pallas_call | solution.py:480
  73.3 0.7 copy.19
  74.1 0.0 copy-done.1
  74.1 0.0 copy-done.6
  74.1 3.1 %shard_map.96 = bf16[3,256,1024]{2,1,0:T(8,128)(2,1)} custom-call(s32[3,2]{1,0:T(4,128)S(1)} %copy.15.owner_ref, s32[16]{0:T(128)S(1)} %copy-done.6, s32[16,8]{1,0:T(8,128)S(1)} %copy.16.path_ref, bf16[3,256,1024]{2,1,0:T(8,128)(2,1)S(1)} %copy-done.1, bf16[3,16,2048]{2,1,0:T(8,128)(2,1)S(1)} %get-tuple-element.5.rows_ref), custom_call_target="tpu_custom_call" | custom-call | tf_op jit(solution)/shard_map/pallas_call | solution.py:522
  (1 shorter events, 0.0 us)
Async XLA Ops:
  2.2 1.4 %copy-start = (bf16[3,256,1024]{2,1,0:T(8,128)(2,1)S(1)}, bf16[3,256,1024]{2,1,0:T(8,128)(2,1)}, u32[]{:S(2)}) copy-start(bf16[3,256,1024]{2,1,0:T(8,128)(2,1)} %cache_ref.3) | copy-start | bytes 4718596
  3.6 1.2 %copy-start.2 = (bf16[2048,256]{1,0:T(8,128)(2,1)S(1)}, bf16[2048,256]{1,0:T(8,128)(2,1)}, u32[]{:S(2)}) copy-start(bf16[2048,256]{1,0:T(8,128)(2,1)} %weight_ref.1) | copy-start | bytes 3145732
  4.8 0.9 %copy-start.3 = (bf16[1,28,2048]{2,1,0:T(8,128)(2,1)S(1)}, bf16[1,28,2048]{2,1,0:T(8,128)(2,1)}, u32[]{:S(2)}) copy-start(bf16[1,28,2048]{2,1,0:T(8,128)(2,1)} %query_ref.1) | copy-start | bytes 344068
  5.7 0.8 %copy-start.4 = (bf16[1,28,1024]{2,1,0:T(8,128)(2,1)S(1)}, bf16[1,28,1024]{2,1,0:T(8,128)(2,1)}, u32[]{:S(2)}) copy-start(bf16[1,28,1024]{2,1,0:T(8,128)(2,1)} %tree_ref.1) | copy-start | bytes 172036
  6.5 0.7 copy-start.5
  7.2 0.7 copy-start.7
  7.8 66.2 %copy-start.1 = (bf16[3,256,1024]{2,1,0:T(8,128)(2,1)S(1)}, bf16[3,256,1024]{2,1,0:T(8,128)(2,1)}, u32[]{:S(2)}) copy-start(bf16[3,256,1024]{2,1,0:T(8,128)(2,1)} %cache_ref.3) | copy-start | bytes 4718596
  7.8 66.2 %copy-start.6 = (s32[16]{0:T(128)S(1)}, s32[16]{0:T(128)}, u32[]{:S(2)}) copy-start(s32[16]{0:T(128)} %len_ref.3) | copy-start | bytes 196

commit v2 on v1

--- a/solution.py
+++ b/solution.py
@@ -139,6 +139,7 @@
 MESH = pl.DeviceIdType.MESH
 PAD = 32
 KINDS = 19
+VMEM_LIMIT = 63 * 1024 * 1024
 
 
 def place():
@@ -149,24 +150,25 @@
 
 
 class GridGather:
-    def __init__(self, buf, send, recv):
+    def __init__(self, buf, send, recv, part):
         me, y, x, planes = place()
-        self.buf, self.send, self.recv = buf, send, recv
+        self.buf, self.send, self.recv, self.part = buf, send, recv, part
         self.column = [plane * 4 + y * 2 + x for plane in planes]
         self.to_x, self.to_y = 1 - 2 * x, 2 - 4 * y
+        self.near_x, self.near_y = me + self.to_x, me + self.to_y
         self.me = me
         self.sent = []
 
-    def copy(self, origin, part, target, kind):
+    def copy(self, origin, piece, target, kind):
         rows = self.buf.shape[1]
         half = rows // 2
-        start, size = {"all": (0, rows), "top": (0, half), "low": (half, half)}[part]
+        start, size = {"all": (0, rows), "top": (0, half), "low": (half, half)}[piece]
         block = self.buf.at[origin, pl.ds(start, size)]
         return pltpu.make_async_remote_copy(
             src_ref=block,
             dst_ref=block,
-            send_sem=self.send.at[kind],
-            recv_sem=self.recv.at[kind],
+            send_sem=self.send.at[self.part, kind],
+            recv_sem=self.recv.at[self.part, kind],
             device_id={"req": target},
             device_id_type=MESH,
         )
@@ -176,27 +178,30 @@
         moving.start()
         self.sent.append(moving)
 
-    def run(self):
-        me, column = self.me, self.column
-        near_x, near_y = me + self.to_x, me + self.to_y
+    def begin(self):
         for k in range(1, 4):
-            self.go(me, "all", column[k], k - 1)
-        for k in range(5):
-            if k < 4:
-                if k:
-                    self.copy(column[k], "all", near_x, k - 1).wait_recv()
-                self.go(column[k], "all", near_x, 3 + k)
-                self.go(column[k], "all", near_y, 7 + k)
+            self.go(self.me, "all", self.column[k], k - 1)
+        self.step(0)
+
+    def step(self, k):
+        column = self.column
+        if k < 4:
             if k:
-                before = column[k - 1]
-                self.copy(before + self.to_x, "all", near_x, 2 + k).wait_recv()
-                self.go(before + self.to_x, "top", near_y, 10 + k)
-                self.copy(before + self.to_y, "all", near_x, 6 + k).wait_recv()
-                self.go(before + self.to_y, "low", near_x, 14 + k)
+                self.copy(column[k], "all", self.near_x, k - 1).wait_recv()
+            self.go(column[k], "all", self.near_x, 3 + k)
+            self.go(column[k], "all", self.near_y, 7 + k)
+        if k:
+            across_x, across_y = column[k - 1] + self.to_x, column[k - 1] + self.to_y
+            self.copy(across_x, "all", self.near_x, 2 + k).wait_recv()
+            self.go(across_x, "top", self.near_y, 10 + k)
+            self.copy(across_y, "all", self.near_x, 6 + k).wait_recv()
+            self.go(across_y, "low", self.near_x, 14 + k)
+
+    def end(self):
         for k in range(4):
-            across = column[k] + self.to_x + self.to_y
-            self.copy(across, "top", near_x, 11 + k).wait_recv()
-            self.copy(across, "low", near_x, 15 + k).wait_recv()
+            across = self.column[k] + self.to_x + self.to_y
+            self.copy(across, "top", self.near_x, 11 + k).wait_recv()
+            self.copy(across, "low", self.near_x, 15 + k).wait_recv()
 
     def finish(self):
         for moving in self.sent:
@@ -247,22 +252,30 @@
 
 
 def layer_kernel(
-    owner_ref, len_ref, parent_ref, path_ref, query_ref, tree_ref, cache_ref, weight_ref,
+    owner_h, len_h, parent_h, path_h, query_h, tree_h, cache_h, weight_h,
     mixed_ref, rows_ref,
-    cache_v, weight_v, gathered, packed, tree_f, tree_b, reach_v, outgoing, incoming,
+    owner_ref, len_ref, parent_ref, path_ref, query_ref, tree_ref, cache_v, weight_v,
+    gathered_a, gathered_b, packed, tree_f, tree_b, reach_v, outgoing, incoming,
     wide, owners, joined, compact, attn, half_out, half_in,
     local_sem, send1, recv1, send2, recv2, send3, recv3, send4, recv4,
 ):
     me, y, x, planes = place()
     tp = lax.axis_index("tp")
-    tree_size = query_ref.shape[1]
-    slots = cache_ref.shape[0]
-    piece_rows = cache_ref.shape[1]
+    gathered = [gathered_a, gathered_b]
+    tree_size = query_h.shape[1]
+    slots = cache_h.shape[0]
+    piece_rows = cache_h.shape[1]
     scaling = 1.0 / math.sqrt(HD)
-    load_cache = pltpu.make_async_copy(cache_ref, cache_v, local_sem.at[0])
-    load_weight = pltpu.make_async_copy(weight_ref, weight_v, local_sem.at[1])
-    load_cache.start()
-    load_weight.start()
+    pairs = [
+        (query_h, query_ref), (tree_h, tree_ref), (path_h, path_ref), (parent_h, parent_ref),
+        (owner_h, owner_ref), (len_h, len_ref), (cache_h, cache_v), (weight_h, weight_v),
+    ]
+    loads = [
+        pltpu.make_async_copy(there, here, local_sem.at[n])
+        for n, (there, here) in enumerate(pairs)
+    ]
+    for load in loads:
+        load.start()
 
     barrier = pltpu.get_barrier_semaphore()
     for d in range(1, 16):
@@ -271,23 +284,33 @@
         )
     pl.semaphore_signal(barrier, inc=1, device_id={"tp": 1 - tp}, device_id_type=MESH)
 
+    for load in loads[:3]:
+        load.wait()
     tree_f[...] = jnp.zeros_like(tree_f)
     tree_f[0:tree_size] = tree_ref[0].astype(jnp.float32)
     tree_b[...] = tree_f[...].astype(jnp.bfloat16)
-    path = as_column(path_ref[pl.ds(me, 1), :].astype(jnp.float32))
+    table = path_ref[...].astype(jnp.float32)
+    path = jnp.sum(jnp.where(iota(table.shape, 1) == me, table, 0.0), axis=1, keepdims=True)
     depth = path.shape[0]
     chosen = (path == iota((depth, PAD), 1).astype(jnp.float32)).astype(jnp.bfloat16)
     picked = jnp.dot(chosen, tree_b[...], preferred_element_type=jnp.float32)
-    width = tree_ref.shape[2]
+    width = tree_h.shape[2]
     packed[0:tree_size] = query_ref[0].astype(jnp.float32)
     packed[tree_size:PAD, 0:width] = picked[0:4]
     packed[tree_size:PAD, width : 2 * width] = picked[4:8]
-    gathered[me] = packed[...].astype(jnp.bfloat16)
+    for c in range(2):
+        gathered[c][me] = packed[:, c * width : (c + 1) * width].astype(jnp.bfloat16)
 
     pl.semaphore_wait(barrier, 16)
-    first = GridGather(gathered, send1, recv1)
-    first.run()
-
+    first = [GridGather(gathered[c], send1, recv1, c) for c in range(2)]
+    first[0].begin()
+    first[0].step(1)
+    first[1].begin()
+    first[0].step(2)
+    first[0].step(3)
+    first[1].step(1)
+
+    loads[3].wait()
     parent = as_column(parent_ref[...].astype(jnp.float32))
     lanes = iota((tree_size, PAD), 1).astype(jnp.float32)
     reach_v[...] = (iota((PAD, PAD), 0) == iota((PAD, PAD), 1)).astype(jnp.float32)
@@ -299,40 +322,42 @@
         short = reached.astype(jnp.bfloat16)
         reached = jnp.minimum(jnp.dot(short, short, preferred_element_type=jnp.float32), 1.0)
     tree_mask = jnp.concatenate([reached] * 4, axis=0) > 0.5
-
-    load_cache.wait()
+    first[0].step(4)
+    first[1].step(2)
+    for load in loads[4:7]:
+        load.wait()
+
     sent = []
-    for k in range(4):
-        plane = planes[k]
+
+    def attend_head(kv):
+        c, offset = kv // 2, (kv % 2) * 4 * HD
         for s in range(slots + 1):
             if s < slots:
-                owner = owner_ref[s, 0]
+                owner = owner_ref[0, s]
                 request = jnp.maximum(owner, 0)
-                limit = jnp.where(owner >= 0, len_ref[request] - owner_ref[s, 1] * piece_rows, 0)
+                limit = jnp.where(owner >= 0, len_ref[request] - owner_ref[1, s] * piece_rows, 0)
                 mask = iota((4 * PAD, piece_rows), 1) < limit
                 source, keys = request, cache_v.at[s]
-                if k == 0:
-                    rows_ref[s] = gathered[request, 16:32, :]
             else:
                 owner, source, keys, mask = me, me, tree_b, tree_mask
-            start = pl.multiple_of(plane * 4 * HD, 4 * HD)
-            wide_q = gathered[source, :, pl.ds(start, 4 * HD)]
+            wide_q = gathered[c][source, :, offset : offset + 4 * HD]
             query = jnp.concatenate([wide_q[:, g * HD : (g + 1) * HD] for g in range(4)], axis=0)
-            at = pl.multiple_of(plane * 2 * HD, 2 * HD)
-            both = keys[:, pl.ds(at, 2 * HD)]
+            at = kv * 2 * HD
             blocks = attend(
-                query, both[:, :HD], both[:, HD:], mask, scaling, owner.astype(jnp.float32)
+                query, keys[:, at : at + HD], keys[:, at + HD : at + 2 * HD], mask, scaling,
+                owner.astype(jnp.float32),
             )
             for g in range(4):
-                outgoing[4 * k + g, s * PAD : (s + 1) * PAD] = blocks[g]
-        for g in range(4):
-            target = plane * 4 + g
-
-            def remote(target=target, n=4 * k + g):
+                outgoing[kv, g, s * PAD : (s + 1) * PAD] = blocks[g]
+        for k in range(4):
+            plane = planes[k]
+            target = plane * 4 + kv
+
+            def remote(target=target, plane=plane, k=k):
                 return pltpu.make_async_remote_copy(
-                    src_ref=outgoing.at[n],
+                    src_ref=outgoing.at[kv, plane],
                     dst_ref=incoming.at[me],
-                    send_sem=send2.at[n],
+                    send_sem=send2.at[kv, k],
                     recv_sem=recv2.at[me],
                     device_id={"req": target},
                     device_id_type=MESH,
@@ -346,17 +371,30 @@
 
                 @pl.when(target == me)
                 def _():
-                    incoming[me] = outgoing[g]
+                    incoming[me] = outgoing[kv, plane]
 
             else:
                 remote().start()
             sent.append((k, target, remote))
+
+    first[0].end()
+    attend_head(0)
+    first[1].step(3)
+    attend_head(1)
+    first[1].step(4)
+    first[1].end()
+    attend_head(2)
+    attend_head(3)
+    for s in range(slots):
+        request = jnp.maximum(owner_ref[0, s], 0)
+        for c in range(2):
+            rows_ref[s, :, c * width : (c + 1) * width] = gathered[c][request, 16:32, :]
     for d in range(1, 16):
         source = (me + d) % 16
         pltpu.make_async_remote_copy(
-            src_ref=outgoing.at[0],
+            src_ref=outgoing.at[0, 0],
             dst_ref=incoming.at[source],
-            send_sem=send2.at[0],
+            send_sem=send2.at[0, 0],
             recv_sem=recv2.at[source],
             device_id={"req": source},
             device_id_type=MESH,
@@ -378,41 +416,56 @@
         block = slice(b * PAD, (b + 1) * PAD)
         wide[block] = wide[block] * turned[0:PAD, b : b + 1]
 
-    def join(r, carry):
-        mine = r.astype(jnp.float32)
-        first_row = pl.multiple_of((r * (slots + 1) + slots) * PAD, PAD)
-        total = wide[pl.ds(first_row, PAD), :]
-        for b in range(pieces):
-            if b % (slots + 1) < slots:
-                total = total + jnp.where(
-                    owners[b : b + 1] == mine, wide[b * PAD : (b + 1) * PAD], 0.0
+    def join_half(part, to):
+        def join(i, carry):
+            r = part * 8 + i
+            mine = r.astype(jnp.float32)
+            first_row = pl.multiple_of((r * (slots + 1) + slots) * PAD, PAD)
+            total = wide[pl.ds(first_row, PAD), :]
+            for b in range(pieces):
+                if b % (slots + 1) < slots:
+                    total = total + jnp.where(
+                        owners[b : b + 1] == mine, wide[b * PAD : (b + 1) * PAD], 0.0
+                    )
+            joined[i] = total
+            return carry
+
+        lax.fori_loop(0, 8, join, 0)
+        for i in range(8):
+            compact[pl.ds(i, tree_size, stride=8), :] = joined[i, 0:tree_size]
+        attn[to, me] = compact[...].astype(jnp.bfloat16)
+
+    last = [GridGather(attn.at[c], send3, recv3, c) for c in range(2)]
+    join_half(1 - tp, 0)
+    last[0].begin()
+    join_half(tp, 1)
+    last[0].step(1)
+    last[1].begin()
+    last[0].step(2)
+    last[1].step(1)
+    last[0].step(3)
+    last[1].step(2)
+    last[0].step(4)
+    last[1].step(3)
+    loads[7].wait()
+
+    def project(part):
+        total = jnp.zeros(half_out.shape, jnp.float32)
+        for kv in range(4):
+            for g in range(0, 4, 2):
+                head = 4 * kv + g
+                pair = jnp.concatenate(
+                    [attn[part, 4 * g + kv], attn[part, 4 * g + 4 + kv]], axis=1
                 )
-        joined[r] = total
-        return carry
-
-    lax.fori_loop(0, 16, join, 0)
-    for r in range(16):
-        compact[r * tree_size : (r + 1) * tree_size] = joined[r, 0:tree_size]
-    attn[me] = compact[...].astype(jnp.bfloat16)
-
-    last = GridGather(attn, send3, recv3)
-    last.run()
-    load_weight.wait()
-    size = half_out.shape[0]
-
-    def project(part):
-        begin = pl.multiple_of(part * size, size)
-        total = jnp.zeros(half_out.shape, jnp.float32)
-        for j in range(0, 16, 2):
-            pair = jnp.concatenate(
-                [attn[j, pl.ds(begin, size), :], attn[j + 1, pl.ds(begin, size), :]], axis=1
-            )
-            total = total + jnp.dot(
-                pair, weight_v[j * HD : (j + 2) * HD], preferred_element_type=jnp.float32
-            )
+                total = total + jnp.dot(
+                    pair, weight_v[head * HD : (head + 2) * HD],
+                    preferred_element_type=jnp.float32,
+                )
         return total
 
-    half_out[...] = project(1 - tp).astype(jnp.bfloat16)
+    last[0].end()
+    last[1].step(4)
+    half_out[...] = project(0).astype(jnp.bfloat16)
     swap = pltpu.make_async_remote_copy(
         src_ref=half_out,
         dst_ref=half_in,
@@ -422,13 +475,14 @@
         device_id_type=MESH,
     )
     swap.start()
-    own_half = project(tp)
+    last[1].end()
+    own_half = project(1)
     swap.wait_recv()
     mixed_ref[...] = (own_half + half_in[...].astype(jnp.float32)).astype(jnp.bfloat16)
 
     swap.wait_send()
-    first.finish()
-    last.finish()
+    for gather in first + last:
+        gather.finish()
     for k, target, remote in sent:
         if k == 0:
 
@@ -440,27 +494,38 @@
             remote().wait_send()
 
 
-def append_kernel(owner_ref, len_ref, path_ref, cache_ref, rows_ref, out_ref):
-    s = pl.program_id(0)
-    owner = owner_ref[s, 0]
-    request = jnp.maximum(owner, 0)
-    piece_rows, width = cache_ref.shape[1], cache_ref.shape[2]
-    count = jnp.int32(0)
-    for j in range(path_ref.shape[1]):
-        count = count + (path_ref[request, j] >= 0).astype(jnp.int32)
-    count = jnp.where(owner >= 0, count, 0)
-    begin = len_ref[request] - owner_ref[s, 1] * piece_rows
-    offset = iota((piece_rows, 16), 0) - begin
-    lane = iota((piece_rows, 16), 1) - 12
-    low = ((offset == lane) & (lane >= 0)).astype(jnp.bfloat16)
-    high = ((offset == lane + 4) & (lane >= 0)).astype(jnp.bfloat16)
-    rows = rows_ref[0]
-    chosen = jnp.dot(low, rows[:, :width], preferred_element_type=jnp.float32) + jnp.dot(
-        high, rows[:, width:], preferred_element_type=jnp.float32
-    )
-    offset = iota((piece_rows, width), 0) - begin
-    writing = (offset >= 0) & (offset < count)
-    out_ref[0] = jnp.where(writing, chosen, cache_ref[0].astype(jnp.float32)).astype(jnp.bfloat16)
+def append_kernel(owner_ref, len_ref, path_ref, cache_ref, rows_ref, out_ref, sems, *held):
+    slots, piece_rows, width = cache_ref.shape
+    span = 32
+    loads = [pltpu.make_async_copy(cache_ref.at[s], held[s], sems.at[s]) for s in range(slots)]
+    stores = [
+        pltpu.make_async_copy(held[s], out_ref.at[s], sems.at[slots + s]) for s in range(slots)
+    ]
+    for load in loads:
+        load.start()
+    for s in range(slots):
+        request = jnp.maximum(owner_ref[0, s], 0)
+        begin = len_ref[request] - owner_ref[1, s] * piece_rows
+        start = pl.multiple_of(jnp.clip(begin, 0, piece_rows - span) // 16 * 16, 16)
+        count = jnp.int32(0)
+        for j in range(path_ref.shape[0]):
+            count = count + (path_ref[j, request] >= 0).astype(jnp.int32)
+        count = jnp.where(owner_ref[0, s] >= 0, count, 0)
+        offset = iota((span, 16), 0) + (start - begin)
+        lane = iota((span, 16), 1) - 12
+        low = ((offset == lane) & (lane >= 0)).astype(jnp.bfloat16)
+        high = ((offset == lane + 4) & (lane >= 0)).astype(jnp.bfloat16)
+        chosen = jnp.dot(
+            low, rows_ref[s, :, :width], preferred_element_type=jnp.float32
+        ) + jnp.dot(high, rows_ref[s, :, width:], preferred_element_type=jnp.float32)
+        offset = iota((span, width), 0) + (start - begin)
+        writing = (offset >= 0) & (offset < count)
+        loads[s].wait()
+        near = held[s][pl.ds(start, span), :].astype(jnp.float32)
+        held[s][pl.ds(start, span), :] = jnp.where(writing, chosen, near).astype(jnp.bfloat16)
+        stores[s].start()
+    for store in stores:
+        store.wait()
 
 
 def shards_grid(
@@ -473,61 +538,67 @@
     half = reqs * tree_size // 2
     smem = pl.BlockSpec(memory_space=pltpu.SMEM)
     vmem = pl.BlockSpec(memory_space=pltpu.VMEM)
-    anywhere = pl.BlockSpec(memory_space=pl.ANY)
+    hbm = pl.BlockSpec(memory_space=pltpu.HBM)
     pieces = reqs * (slots + 1)
     dma = pltpu.SemaphoreType.DMA
-    bf16, f32 = jnp.bfloat16, jnp.float32
+    bf16, f32, i32 = jnp.bfloat16, jnp.float32, jnp.int32
+    owner_t, path_t = piece_owner.T, accepted_path.T
     mixed, rows = pl.pallas_call(
         layer_kernel,
         out_shape=(
             jax.ShapeDtypeStruct((half, out_weight.shape[1]), bf16),
             jax.ShapeDtypeStruct((slots, 16, columns), bf16),
         ),
-        in_specs=[smem, smem, vmem, vmem, vmem, vmem, anywhere, anywhere],
+        in_specs=[hbm] * 8,
         out_specs=(vmem, vmem),
         scratch_shapes=[
+            pltpu.SMEM(owner_t.shape, i32),
+            pltpu.SMEM(cache_len.shape, i32),
+            pltpu.VMEM(tree_parent.shape, i32),
+            pltpu.VMEM(path_t.shape, i32),
+            pltpu.VMEM(queries.shape, bf16),
+            pltpu.VMEM(tree_kv.shape, bf16),
             pltpu.VMEM(cache_kv.shape, bf16),
             pltpu.VMEM(out_weight.shape, bf16),
-            pltpu.VMEM((reqs, PAD, columns), bf16),
+            pltpu.VMEM((reqs, PAD, columns // 2), bf16),
+            pltpu.VMEM((reqs, PAD, columns // 2), bf16),
             pltpu.VMEM((PAD, columns), f32),
             pltpu.VMEM((PAD, width), f32),
             pltpu.VMEM((PAD, width), bf16),
             pltpu.VMEM((PAD, PAD), f32),
-            pltpu.VMEM((reqs, (slots + 1) * PAD, HD), bf16),
+            pltpu.VMEM((4, 4, (slots + 1) * PAD, HD), bf16),
             pltpu.VMEM((reqs, (slots + 1) * PAD, HD), bf16),
             pltpu.VMEM((pieces * PAD, HD), f32),
             pltpu.VMEM((pieces, HD), f32),
-            pltpu.VMEM((reqs, PAD, HD), f32),
-            pltpu.VMEM((reqs * tree_size, HD), f32),
-            pltpu.VMEM((reqs, reqs * tree_size, HD), bf16),
+            pltpu.VMEM((reqs // 2, PAD, HD), f32),
+            pltpu.VMEM((half, HD), f32),
+            pltpu.VMEM((2, reqs, half, HD), bf16),
             pltpu.VMEM((half, out_weight.shape[1]), bf16),
             pltpu.VMEM((half, out_weight.shape[1]), bf16),
-            dma((2,)),
-            dma((KINDS,)),
-            dma((KINDS,)),
+            dma((8,)),
+            dma((2, KINDS)),
+            dma((2, KINDS)),
+            dma((4, 4)),
             dma((reqs,)),
-            dma((reqs,)),
-            dma((KINDS,)),
-            dma((KINDS,)),
+            dma((2, KINDS)),
+            dma((2, KINDS)),
             dma,
             dma,
         ],
         compiler_params=pltpu.CompilerParams(
-            collective_id=0, has_side_effects=True, vmem_limit_bytes=48 * 1024 * 1024
+            collective_id=0, has_side_effects=True, vmem_limit_bytes=VMEM_LIMIT
         ),
-    )(
-        piece_owner, cache_len, tree_parent, accepted_path, queries, tree_kv, cache_kv, out_weight
-    )
-    block = pl.BlockSpec((1, piece_rows, width), lambda s: (s, 0, 0))
+    )(owner_t, cache_len, tree_parent, path_t, queries, tree_kv, cache_kv, out_weight)
     cache_out = pl.pallas_call(
         append_kernel,
         out_shape=jax.ShapeDtypeStruct(cache_kv.shape, bf16),
-        grid=(slots,),
-        in_specs=[smem, smem, smem, block, pl.BlockSpec((1, 16, columns), lambda s: (s, 0, 0))],
-        out_specs=block,
-        compiler_params=pltpu.CompilerParams(vmem_limit_bytes=32 * 1024 * 1024),
-    )(piece_owner, cache_len, accepted_path, cache_kv, rows)
-    return mixed.reshape(reqs // 2, tree_size, out_weight.shape[1]), cache_out
+        in_specs=[smem, smem, smem, hbm, vmem],
+        out_specs=hbm,
+        scratch_shapes=[dma((2 * slots,))] + [pltpu.VMEM(cache_kv.shape[1:], bf16)] * slots,
+        compiler_params=pltpu.CompilerParams(vmem_limit_bytes=VMEM_LIMIT),
+    )(owner_t, cache_len, path_t, cache_kv, rows)
+    mixed = mixed.reshape(tree_size, reqs // 2, out_weight.shape[1]).transpose(1, 0, 2)
+    return mixed, cache_out
 
 
 def solution(mesh):

time: 77.5 us -> 70.7 us (0.912)
  local copies, waits for them, and re-layouts: 7.95 us -> 0.65 us
    unnamed x19 -> x3, local copies, waits for them, and re-layouts: 7.93 us -> 0.65 us
where the time goes in v2:
time: 70.7 us; the launch traced here: 70.5 us
  Pallas kernels  69.2 us (98%)
    pallas_call x1, Pallas kernels, shards_grid(): pl.pallas_call(layer_kernel, out_shape=(jax.ShapeDtypeStruct((half, out_w...  65.9 us
    pallas_call x1, Pallas kernels, shards_grid(): pl.pallas_call(append_kernel, out_shape=jax.ShapeDtypeStruct(cache_kv.sha...  3.29 us

profile of v2, /device:TPU:0, one launch (start us, length us, event | category | flops | bytes accessed | tf_op | source)
XLA Modules:
  0.0 70.5 jit_solution(2612856576886610423)
XLA Ops:
  0.6 65.9 %shard_map.95 = (bf16[224,256]{1,0:T(8,128)(2,1)}, bf16[3,16,2048]{2,1,0:T(8,128)(2,1)}) custom-call(s32[2,3]{1,0:T(2,128)} %bitcast.8, s32[16]{0:T(128)} %len_ref.1, s32[1,28]{1,0:T(1,128)} %parent_h.1, s32[8,16]{1,0:T(8,128)} %bitcast.6, bf16[1,28,2048]{2,1,0:T(8,128)(2,1)} %query_h.1, bf16[1,28,1024]{2,1,0:T(8,128)(2,1)} %tree_h.1, ...), custom_call_target="tpu_custom_call" | custom-call | tf_op jit(solution)/shard_map/pallas_call | solution.py:546
  66.6 0.0 copy-start
  66.6 3.3 %shard_map.96 = bf16[3,256,1024]{2,1,0:T(8,128)(2,1)} custom-call(s32[2,3]{1,0:T(2,128)} %bitcast.9, s32[16]{0:T(128)} %len_ref.1, s32[8,16]{1,0:T(8,128)} %bitcast.7, bf16[3,256,1024]{2,1,0:T(8,128)(2,1)} %cache_ref.1, bf16[3,16,2048]{2,1,0:T(8,128)(2,1)} %get-tuple-element.5.rows_ref), custom_call_target="tpu_custom_call" | custom-call | tf_op jit(solution)/shard_map/pallas_call | solution.py:592
  69.9 0.0 copy-done
  69.9 0.6 copy.11
Async XLA Ops:
  66.6 3.3 %copy-start = (bf16[224,256]{1,0:T(8,128)(2,1)S(1)}, bf16[224,256]{1,0:T(8,128)(2,1)}, u32[]{:S(2)}) copy-start(bf16[224,256]{1,0:T(8,128)(2,1)} %get-tuple-element.4) | copy-start | bytes 344068

commit v3 on v2

--- a/solution.py
+++ b/solution.py
@@ -138,7 +138,7 @@
 
 MESH = pl.DeviceIdType.MESH
 PAD = 32
-KINDS = 19
+KINDS = 21
 VMEM_LIMIT = 63 * 1024 * 1024
 
 
@@ -149,17 +149,25 @@
     return me, y, x, planes
 
 
+def arrivals():
+    z = lax.axis_index("req") // 4
+    return [z, z + 1 - 2 * (z % 2), 2 - z // 2, 3 - 3 * (z // 2)]
+
+
 class GridGather:
     def __init__(self, buf, send, recv, part):
         me, y, x, planes = place()
         self.buf, self.send, self.recv, self.part = buf, send, recv, part
-        self.column = [plane * 4 + y * 2 + x for plane in planes]
+        self.column = [plane * 4 + y * 2 + x for plane in arrivals()]
+        z = me // 4
+        self.inner = (z + 1) // 2 == 1
+        self.middle = (3 - z) * 4 + y * 2 + x
         self.to_x, self.to_y = 1 - 2 * x, 2 - 4 * y
         self.near_x, self.near_y = me + self.to_x, me + self.to_y
         self.me = me
         self.sent = []
 
-    def copy(self, origin, piece, target, kind):
+    def copy(self, origin, piece, target, kind, arrive=None):
         rows = self.buf.shape[1]
         half = rows // 2
         start, size = {"all": (0, rows), "top": (0, half), "low": (half, half)}[piece]
@@ -168,7 +176,7 @@
             src_ref=block,
             dst_ref=block,
             send_sem=self.send.at[self.part, kind],
-            recv_sem=self.recv.at[self.part, kind],
+            recv_sem=self.recv.at[self.part, kind if arrive is None else arrive],
             device_id={"req": target},
             device_id_type=MESH,
         )
@@ -176,11 +184,18 @@
     def go(self, *args):
         moving = self.copy(*args)
         moving.start()
-        self.sent.append(moving)
+        self.sent.append((None, moving))
+
+    def relay(self, *args):
+        @pl.when(self.inner)
+        def _():
+            self.copy(*args).start()
+
+        self.sent.append((self.inner, args))
 
     def begin(self):
-        for k in range(1, 4):
-            self.go(self.me, "all", self.column[k], k - 1)
+        self.go(self.me, "all", self.column[1], 0, 0)
+        self.relay(self.me, "all", self.middle, 1, 1)
         self.step(0)
 
     def step(self, k):
@@ -188,24 +203,34 @@
         if k < 4:
             if k:
                 self.copy(column[k], "all", self.near_x, k - 1).wait_recv()
-            self.go(column[k], "all", self.near_x, 3 + k)
-            self.go(column[k], "all", self.near_y, 7 + k)
+                if k == 1:
+                    self.relay(column[1], "all", self.middle, 2, 2)
+                else:
+                    self.relay(column[k], "all", column[1], k + 1, k - 1)
+            self.go(column[k], "all", self.near_x, 5 + k)
+            self.go(column[k], "all", self.near_y, 9 + k)
         if k:
             across_x, across_y = column[k - 1] + self.to_x, column[k - 1] + self.to_y
-            self.copy(across_x, "all", self.near_x, 2 + k).wait_recv()
-            self.go(across_x, "top", self.near_y, 10 + k)
-            self.copy(across_y, "all", self.near_x, 6 + k).wait_recv()
-            self.go(across_y, "low", self.near_x, 14 + k)
+            self.copy(across_x, "all", self.near_x, 4 + k).wait_recv()
+            self.go(across_x, "top", self.near_y, 12 + k)
+            self.copy(across_y, "all", self.near_x, 8 + k).wait_recv()
+            self.go(across_y, "low", self.near_x, 16 + k)
 
     def end(self):
         for k in range(4):
             across = self.column[k] + self.to_x + self.to_y
-            self.copy(across, "top", self.near_x, 11 + k).wait_recv()
-            self.copy(across, "low", self.near_x, 15 + k).wait_recv()
+            self.copy(across, "top", self.near_x, 13 + k).wait_recv()
+            self.copy(across, "low", self.near_x, 17 + k).wait_recv()
 
     def finish(self):
-        for moving in self.sent:
-            moving.wait_send()
+        for only, moving in self.sent:
+            if only is None:
+                moving.wait_send()
+                continue
+
+            @pl.when(only)
+            def _():
+                self.copy(*moving).wait_send()
 
 
 def iota(shape, dim):
@@ -253,8 +278,8 @@
 
 def layer_kernel(
     owner_h, len_h, parent_h, path_h, query_h, tree_h, cache_h, weight_h,
-    mixed_ref, rows_ref,
-    owner_ref, len_ref, parent_ref, path_ref, query_ref, tree_ref, cache_v, weight_v,
+    mixed_ref, cache_out,
+    owner_ref, len_ref, parent_ref, path_ref, path_s, query_ref, tree_ref, cache_v, weight_v,
     gathered_a, gathered_b, packed, tree_f, tree_b, reach_v, outgoing, incoming,
     wide, owners, joined, compact, attn, half_out, half_in,
     local_sem, send1, recv1, send2, recv2, send3, recv3, send4, recv4,
@@ -269,6 +294,7 @@
     pairs = [
         (query_h, query_ref), (tree_h, tree_ref), (path_h, path_ref), (parent_h, parent_ref),
         (owner_h, owner_ref), (len_h, len_ref), (cache_h, cache_v), (weight_h, weight_v),
+        (path_h, path_s),
     ]
     loads = [
         pltpu.make_async_copy(there, here, local_sem.at[n])
@@ -385,10 +411,34 @@
     first[1].end()
     attend_head(2)
     attend_head(3)
+    loads[8].wait()
+    saves = [
+        pltpu.make_async_copy(cache_v.at[s], cache_out.at[s], local_sem.at[9 + s])
+        for s in range(slots)
+    ]
+    span = 64
     for s in range(slots):
-        request = jnp.maximum(owner_ref[0, s], 0)
-        for c in range(2):
-            rows_ref[s, :, c * width : (c + 1) * width] = gathered[c][request, 16:32, :]
+        owner = owner_ref[0, s]
+        request = jnp.maximum(owner, 0)
+        begin = len_ref[request] - owner_ref[1, s] * piece_rows
+        count = jnp.int32(0)
+        for j in range(depth):
+            count = count + (path_s[j, request] >= 0).astype(jnp.int32)
+        count = jnp.where(owner >= 0, count, 0)
+        spare = [gathered[c][request, 16:32, :] for c in range(2)]
+        for row in range(0, piece_rows, span):
+            offset = iota((span, 16), 0) + (row - begin)
+            lane = iota((span, 16), 1) - 12
+            low = ((offset == lane) & (lane >= 0)).astype(jnp.bfloat16)
+            high = ((offset == lane + 4) & (lane >= 0)).astype(jnp.bfloat16)
+            accepted = jnp.dot(
+                low, spare[0], preferred_element_type=jnp.float32
+            ) + jnp.dot(high, spare[1], preferred_element_type=jnp.float32)
+            offset = iota((span, width), 0) + (row - begin)
+            writing = (offset >= 0) & (offset < count)
+            old = cache_v[s, row : row + span, :].astype(jnp.float32)
+            cache_v[s, row : row + span, :] = jnp.where(writing, accepted, old).astype(jnp.bfloat16)
+        saves[s].start()
     for d in range(1, 16):
         source = (me + d) % 16
         pltpu.make_async_remote_copy(
@@ -481,6 +531,8 @@
     mixed_ref[...] = (own_half + half_in[...].astype(jnp.float32)).astype(jnp.bfloat16)
 
     swap.wait_send()
+    for save in saves:
+        save.wait()
     for gather in first + last:
         gather.finish()
     for k, target, remote in sent:
@@ -492,40 +544,6 @@
 
         else:
             remote().wait_send()
-
-
-def append_kernel(owner_ref, len_ref, path_ref, cache_ref, rows_ref, out_ref, sems, *held):
-    slots, piece_rows, width = cache_ref.shape
-    span = 32
-    loads = [pltpu.make_async_copy(cache_ref.at[s], held[s], sems.at[s]) for s in range(slots)]
-    stores = [
-        pltpu.make_async_copy(held[s], out_ref.at[s], sems.at[slots + s]) for s in range(slots)
-    ]
-    for load in loads:
-        load.start()
-    for s in range(slots):
-        request = jnp.maximum(owner_ref[0, s], 0)
-        begin = len_ref[request] - owner_ref[1, s] * piece_rows
-        start = pl.multiple_of(jnp.clip(begin, 0, piece_rows - span) // 16 * 16, 16)
-        count = jnp.int32(0)
-        for j in range(path_ref.shape[0]):
-            count = count + (path_ref[j, request] >= 0).astype(jnp.int32)
-        count = jnp.where(owner_ref[0, s] >= 0, count, 0)
-        offset = iota((span, 16), 0) + (start - begin)
-        lane = iota((span, 16), 1) - 12
-        low = ((offset == lane) & (lane >= 0)).astype(jnp.bfloat16)
-        high = ((offset == lane + 4) & (lane >= 0)).astype(jnp.bfloat16)
-        chosen = jnp.dot(
-            low, rows_ref[s, :, :width], preferred_element_type=jnp.float32
-        ) + jnp.dot(high, rows_ref[s, :, width:], preferred_element_type=jnp.float32)
-        offset = iota((span, width), 0) + (start - begin)
-        writing = (offset >= 0) & (offset < count)
-        loads[s].wait()
-        near = held[s][pl.ds(start, span), :].astype(jnp.float32)
-        held[s][pl.ds(start, span), :] = jnp.where(writing, chosen, near).astype(jnp.bfloat16)
-        stores[s].start()
-    for store in stores:
-        store.wait()
 
 
 def shards_grid(
@@ -536,26 +554,26 @@
     columns = queries.shape[2]
     reqs = 16
     half = reqs * tree_size // 2
-    smem = pl.BlockSpec(memory_space=pltpu.SMEM)
     vmem = pl.BlockSpec(memory_space=pltpu.VMEM)
     hbm = pl.BlockSpec(memory_space=pltpu.HBM)
     pieces = reqs * (slots + 1)
     dma = pltpu.SemaphoreType.DMA
     bf16, f32, i32 = jnp.bfloat16, jnp.float32, jnp.int32
     owner_t, path_t = piece_owner.T, accepted_path.T
-    mixed, rows = pl.pallas_call(
+    mixed, cache_out = pl.pallas_call(
         layer_kernel,
         out_shape=(
             jax.ShapeDtypeStruct((half, out_weight.shape[1]), bf16),
-            jax.ShapeDtypeStruct((slots, 16, columns), bf16),
+            jax.ShapeDtypeStruct(cache_kv.shape, bf16),
         ),
         in_specs=[hbm] * 8,
-        out_specs=(vmem, vmem),
+        out_specs=(vmem, hbm),
         scratch_shapes=[
             pltpu.SMEM(owner_t.shape, i32),
             pltpu.SMEM(cache_len.shape, i32),
             pltpu.VMEM(tree_parent.shape, i32),
             pltpu.VMEM(path_t.shape, i32),
+            pltpu.SMEM(path_t.shape, i32),
             pltpu.VMEM(queries.shape, bf16),
             pltpu.VMEM(tree_kv.shape, bf16),
             pltpu.VMEM(cache_kv.shape, bf16),
@@ -575,7 +593,7 @@
             pltpu.VMEM((2, reqs, half, HD), bf16),
             pltpu.VMEM((half, out_weight.shape[1]), bf16),
             pltpu.VMEM((half, out_weight.shape[1]), bf16),
-            dma((8,)),
+            dma((9 + slots,)),
             dma((2, KINDS)),
             dma((2, KINDS)),
             dma((4, 4)),
@@ -589,14 +607,6 @@
             collective_id=0, has_side_effects=True, vmem_limit_bytes=VMEM_LIMIT
         ),
     )(owner_t, cache_len, tree_parent, path_t, queries, tree_kv, cache_kv, out_weight)
-    cache_out = pl.pallas_call(
-        append_kernel,
-        out_shape=jax.ShapeDtypeStruct(cache_kv.shape, bf16),
-        in_specs=[smem, smem, smem, hbm, vmem],
-        out_specs=hbm,
-        scratch_shapes=[dma((2 * slots,))] + [pltpu.VMEM(cache_kv.shape[1:], bf16)] * slots,
-        compiler_params=pltpu.CompilerParams(vmem_limit_bytes=VMEM_LIMIT),
-    )(owner_t, cache_len, path_t, cache_kv, rows)
     mixed = mixed.reshape(tree_size, reqs // 2, out_weight.shape[1]).transpose(1, 0, 2)
     return mixed, cache_out
 

time: 70.7 us -> 73.4 us (1.038)
  local copies, waits for them, and re-layouts: 0.65 us -> 4.22 us
  Pallas kernels: 69.2 us -> 68.3 us
    unnamed x3 -> x2, local copies, waits for them, and re-layouts: 0.65 us -> 4.22 us
    pallas_call x1 -> x0, Pallas kernels: 3.29 us -> none  [shards_grid(): pl.pallas_call(append_kernel, out_shape=jax.ShapeDtypeStruct(cache_kv.sha...]
    pallas_call x1, Pallas kernels: 65.9 us -> 68.3 us  [shards_grid(): pl.pallas_call(layer_kernel, out_shape=(jax.ShapeDtypeStruct((half, out_w...]
where the time goes in v3:
time: 73.4 us; the launch traced here: 73.2 us
  Pallas kernels  68.3 us (93%)
  local copies, waits for them, and re-layouts  4.22 us (6%)
    pallas_call x1, Pallas kernels, shards_grid(): pl.pallas_call(layer_kernel, out_shape=(jax.ShapeDtypeStruct((half, out_w...  68.3 us
    unnamed x2, local copies, waits for them, and re-layouts  4.22 us

profile of v3, /device:TPU:0, one launch (start us, length us, event | category | flops | bytes accessed | tf_op | source)
XLA Modules:
  0.0 73.2 jit_solution(3279001166685191216)
XLA Ops:
  0.6 68.3 %shard_map.95 = (bf16[224,256]{1,0:T(8,128)(2,1)}, bf16[3,256,1024]{2,1,0:T(8,128)(2,1)}) custom-call(s32[2,3]{1,0:T(2,128)} %bitcast.7, s32[16]{0:T(128)} %len_h.1, s32[1,28]{1,0:T(1,128)} %parent_h.1, s32[8,16]{1,0:T(8,128)} %bitcast.6, bf16[1,28,2048]{2,1,0:T(8,128)(2,1)} %query_h.1, bf16[1,28,1024]{2,1,0:T(8,128)(2,1)} %tree_h.1, ...), custom_call_target="tpu_custom_call" | custom-call | tf_op jit(solution)/shard_map/pallas_call | solution.py:563
  69.0 1.6 %copy.12 = bf16[8,28,256]{2,0,1:T(8,128)(2,1)} copy(bf16[8,28,256]{2,0,1:T(8,128)(2,1)} %bitcast.5) | data formatting | bytes 229376
  70.5 2.7 %copy.13 = bf16[3,256,1024]{2,1,0:T(8,128)(2,1)} copy(bf16[3,256,1024]{2,1,0:T(8,128)(2,1)} %get-tuple-element.9) | data formatting | bytes 3145728

commit v4 on v2

--- a/solution.py
+++ b/solution.py
@@ -138,7 +138,7 @@
 
 MESH = pl.DeviceIdType.MESH
 PAD = 32
-KINDS = 19
+KINDS = 21
 VMEM_LIMIT = 63 * 1024 * 1024
 
 
@@ -149,17 +149,25 @@
     return me, y, x, planes
 
 
+def arrivals():
+    z = lax.axis_index("req") // 4
+    return [z, z + 1 - 2 * (z % 2), 2 - z // 2, 3 - 3 * (z // 2)]
+
+
 class GridGather:
     def __init__(self, buf, send, recv, part):
         me, y, x, planes = place()
         self.buf, self.send, self.recv, self.part = buf, send, recv, part
-        self.column = [plane * 4 + y * 2 + x for plane in planes]
+        self.column = [plane * 4 + y * 2 + x for plane in arrivals()]
+        z = me // 4
+        self.inner = (z + 1) // 2 == 1
+        self.middle = (3 - z) * 4 + y * 2 + x
         self.to_x, self.to_y = 1 - 2 * x, 2 - 4 * y
         self.near_x, self.near_y = me + self.to_x, me + self.to_y
         self.me = me
         self.sent = []
 
-    def copy(self, origin, piece, target, kind):
+    def copy(self, origin, piece, target, kind, arrive=None):
         rows = self.buf.shape[1]
         half = rows // 2
         start, size = {"all": (0, rows), "top": (0, half), "low": (half, half)}[piece]
@@ -168,7 +176,7 @@
             src_ref=block,
             dst_ref=block,
             send_sem=self.send.at[self.part, kind],
-            recv_sem=self.recv.at[self.part, kind],
+            recv_sem=self.recv.at[self.part, kind if arrive is None else arrive],
             device_id={"req": target},
             device_id_type=MESH,
         )
@@ -176,11 +184,18 @@
     def go(self, *args):
         moving = self.copy(*args)
         moving.start()
-        self.sent.append(moving)
+        self.sent.append((None, moving))
+
+    def relay(self, *args):
+        @pl.when(self.inner)
+        def _():
+            self.copy(*args).start()
+
+        self.sent.append((self.inner, args))
 
     def begin(self):
-        for k in range(1, 4):
-            self.go(self.me, "all", self.column[k], k - 1)
+        self.go(self.me, "all", self.column[1], 0, 0)
+        self.relay(self.me, "all", self.middle, 1, 1)
         self.step(0)
 
     def step(self, k):
@@ -188,24 +203,34 @@
         if k < 4:
             if k:
                 self.copy(column[k], "all", self.near_x, k - 1).wait_recv()
-            self.go(column[k], "all", self.near_x, 3 + k)
-            self.go(column[k], "all", self.near_y, 7 + k)
+                if k == 1:
+                    self.relay(column[1], "all", self.middle, 2, 2)
+                else:
+                    self.relay(column[k], "all", column[1], k + 1, k - 1)
+            self.go(column[k], "all", self.near_x, 5 + k)
+            self.go(column[k], "all", self.near_y, 9 + k)
         if k:
             across_x, across_y = column[k - 1] + self.to_x, column[k - 1] + self.to_y
-            self.copy(across_x, "all", self.near_x, 2 + k).wait_recv()
-            self.go(across_x, "top", self.near_y, 10 + k)
-            self.copy(across_y, "all", self.near_x, 6 + k).wait_recv()
-            self.go(across_y, "low", self.near_x, 14 + k)
+            self.copy(across_x, "all", self.near_x, 4 + k).wait_recv()
+            self.go(across_x, "top", self.near_y, 12 + k)
+            self.copy(across_y, "all", self.near_x, 8 + k).wait_recv()
+            self.go(across_y, "low", self.near_x, 16 + k)
 
     def end(self):
         for k in range(4):
             across = self.column[k] + self.to_x + self.to_y
-            self.copy(across, "top", self.near_x, 11 + k).wait_recv()
-            self.copy(across, "low", self.near_x, 15 + k).wait_recv()
+            self.copy(across, "top", self.near_x, 13 + k).wait_recv()
+            self.copy(across, "low", self.near_x, 17 + k).wait_recv()
 
     def finish(self):
-        for moving in self.sent:
-            moving.wait_send()
+        for only, moving in self.sent:
+            if only is None:
+                moving.wait_send()
+                continue
+
+            @pl.when(only)
+            def _():
+                self.copy(*moving).wait_send()
 
 
 def iota(shape, dim):
@@ -254,14 +279,13 @@
 def layer_kernel(
     owner_h, len_h, parent_h, path_h, query_h, tree_h, cache_h, weight_h,
     mixed_ref, rows_ref,
-    owner_ref, len_ref, parent_ref, path_ref, query_ref, tree_ref, cache_v, weight_v,
-    gathered_a, gathered_b, packed, tree_f, tree_b, reach_v, outgoing, incoming,
+    owner_ref, owner_v, len_ref, parent_ref, path_ref, query_ref, tree_ref, cache_v, weight_v,
+    own_heads, owned, known_v, known, staged, asked, packed, tree_f, tree_b, reach_v, outgoing, incoming,
     wide, owners, joined, compact, attn, half_out, half_in,
-    local_sem, send1, recv1, send2, recv2, send3, recv3, send4, recv4,
+    local_sem, send0, recv0, send5, recv5, send1, recv1, send2, recv2, send3, recv3, send4, recv4,
 ):
     me, y, x, planes = place()
     tp = lax.axis_index("tp")
-    gathered = [gathered_a, gathered_b]
     tree_size = query_h.shape[1]
     slots = cache_h.shape[0]
     piece_rows = cache_h.shape[1]
@@ -269,6 +293,7 @@
     pairs = [
         (query_h, query_ref), (tree_h, tree_ref), (path_h, path_ref), (parent_h, parent_ref),
         (owner_h, owner_ref), (len_h, len_ref), (cache_h, cache_v), (weight_h, weight_v),
+        (owner_h, owner_v),
     ]
     loads = [
         pltpu.make_async_copy(there, here, local_sem.at[n])
@@ -284,7 +309,7 @@
         )
     pl.semaphore_signal(barrier, inc=1, device_id={"tp": 1 - tp}, device_id_type=MESH)
 
-    for load in loads[:3]:
+    for load in loads[:3] + loads[8:9]:
         load.wait()
     tree_f[...] = jnp.zeros_like(tree_f)
     tree_f[0:tree_size] = tree_ref[0].astype(jnp.float32)
@@ -298,17 +323,48 @@
     packed[0:tree_size] = query_ref[0].astype(jnp.float32)
     packed[tree_size:PAD, 0:width] = picked[0:4]
     packed[tree_size:PAD, width : 2 * width] = picked[4:8]
-    for c in range(2):
-        gathered[c][me] = packed[:, c * width : (c + 1) * width].astype(jnp.bfloat16)
+    for head in range(16):
+        device = 4 * (head % 4) + head // 4
+        own_heads[device] = packed[:, head * HD : (head + 1) * HD].astype(jnp.bfloat16)
+    owned[me] = own_heads[me]
+    known_v[me] = jnp.zeros(known_v.shape[1:], jnp.int32)
+    known_v[me, 0:1, 0:slots] = owner_v[0:1, :]
 
     pl.semaphore_wait(barrier, 16)
-    first = [GridGather(gathered[c], send1, recv1, c) for c in range(2)]
-    first[0].begin()
-    first[0].step(1)
-    first[1].begin()
-    first[0].step(2)
-    first[0].step(3)
-    first[1].step(1)
+
+    others = []
+    for k in range(4):
+        for c in range(4):
+            others.append((planes[k] * 4 + (me + c) % 4, k + c > 0))
+    others = [device for device, other in others if other]
+    hops = []
+
+    def post(block, to, target, send, recv, n):
+        moving = pltpu.make_async_remote_copy(
+            src_ref=block,
+            dst_ref=to,
+            send_sem=send.at[n],
+            recv_sem=recv.at[me],
+            device_id={"req": target},
+            device_id_type=MESH,
+        )
+        moving.start()
+        hops.append(moving)
+
+    def take(block, send, recv, source):
+        pltpu.make_async_remote_copy(
+            src_ref=block,
+            dst_ref=block,
+            send_sem=send.at[0],
+            recv_sem=recv.at[source],
+            device_id={"req": (me + 1) % 16},
+            device_id_type=MESH,
+        ).wait_recv()
+
+    for n, target in enumerate(others):
+        post(known_v.at[me], known_v.at[me], target, send0, recv0, n)
+    for n, target in enumerate(others):
+        post(own_heads.at[target], owned.at[me], target, send1, recv1, n)
 
     loads[3].wait()
     parent = as_column(parent_ref[...].astype(jnp.float32))
@@ -322,26 +378,48 @@
         short = reached.astype(jnp.bfloat16)
         reached = jnp.minimum(jnp.dot(short, short, preferred_element_type=jnp.float32), 1.0)
     tree_mask = jnp.concatenate([reached] * 4, axis=0) > 0.5
-    first[0].step(4)
-    first[1].step(2)
     for load in loads[4:7]:
         load.wait()
+    for source in others:
+        take(known_v.at[source], send0, recv0, source)
+    table = pltpu.make_async_copy(known_v, known, local_sem.at[9])
+    table.start()
+    table.wait()
+    for source in others:
+        take(owned.at[source], send1, recv1, source)
+
+    def stage(device, to):
+        for s in range(slots):
+            request = jnp.maximum(known[device, 0, s], 0)
+            to[s * PAD : (s + 1) * PAD] = owned[request]
+
+    for n, target in enumerate(others):
+        stage(target, staged.at[n])
+        post(staged.at[n], asked.at[me], target, send5, recv5, n)
+    stage(me, asked.at[me])
 
     sent = []
 
     def attend_head(kv):
-        c, offset = kv // 2, (kv % 2) * 4 * HD
+        for g in range(4):
+            source = 4 * g + kv
+
+            @pl.when(source != me)
+            def _():
+                take(asked.at[source], send5, recv5, source)
+
         for s in range(slots + 1):
             if s < slots:
                 owner = owner_ref[0, s]
                 request = jnp.maximum(owner, 0)
                 limit = jnp.where(owner >= 0, len_ref[request] - owner_ref[1, s] * piece_rows, 0)
                 mask = iota((4 * PAD, piece_rows), 1) < limit
-                source, keys = request, cache_v.at[s]
+                keys = cache_v.at[s]
+                parts = [asked[4 * g + kv, s * PAD : (s + 1) * PAD, :] for g in range(4)]
             else:
-                owner, source, keys, mask = me, me, tree_b, tree_mask
-            wide_q = gathered[c][source, :, offset : offset + 4 * HD]
-            query = jnp.concatenate([wide_q[:, g * HD : (g + 1) * HD] for g in range(4)], axis=0)
+                owner, keys, mask = me, tree_b, tree_mask
+                parts = [own_heads[4 * g + kv] for g in range(4)]
+            query = jnp.concatenate(parts, axis=0)
             at = kv * 2 * HD
             blocks = attend(
                 query, keys[:, at : at + HD], keys[:, at + HD : at + 2 * HD], mask, scaling,
@@ -377,18 +455,14 @@
                 remote().start()
             sent.append((k, target, remote))
 
-    first[0].end()
-    attend_head(0)
-    first[1].step(3)
-    attend_head(1)
-    first[1].step(4)
-    first[1].end()
-    attend_head(2)
-    attend_head(3)
+    for kv in range(4):
+        attend_head(kv)
     for s in range(slots):
-        request = jnp.maximum(owner_ref[0, s], 0)
-        for c in range(2):
-            rows_ref[s, :, c * width : (c + 1) * width] = gathered[c][request, 16:32, :]
+        for head in range(16):
+            device = 4 * (head % 4) + head // 4
+            rows_ref[s, :, head * HD : (head + 1) * HD] = asked[
+                device, s * PAD + 16 : (s + 1) * PAD, :
+            ]
     for d in range(1, 16):
         source = (me + d) % 16
         pltpu.make_async_remote_copy(
@@ -481,7 +555,9 @@
     mixed_ref[...] = (own_half + half_in[...].astype(jnp.float32)).astype(jnp.bfloat16)
 
     swap.wait_send()
-    for gather in first + last:
+    for hop in hops:
+        hop.wait_send()
+    for gather in last:
         gather.finish()
     for k, target, remote in sent:
         if k == 0:
@@ -494,15 +570,25 @@
             remote().wait_send()
 
 
-def append_kernel(owner_ref, len_ref, path_ref, cache_ref, rows_ref, out_ref, sems, *held):
+def append_kernel(
+    owner_h, len_h, path_h, cache_ref, rows_h, out_ref,
+    owner_ref, len_ref, path_ref, rows_ref, sems, *held,
+):
     slots, piece_rows, width = cache_ref.shape
     span = 32
     loads = [pltpu.make_async_copy(cache_ref.at[s], held[s], sems.at[s]) for s in range(slots)]
     stores = [
         pltpu.make_async_copy(held[s], out_ref.at[s], sems.at[slots + s]) for s in range(slots)
     ]
-    for load in loads:
+    pairs = [(owner_h, owner_ref), (len_h, len_ref), (path_h, path_ref), (rows_h, rows_ref)]
+    small = [
+        pltpu.make_async_copy(there, here, sems.at[2 * slots + n])
+        for n, (there, here) in enumerate(pairs)
+    ]
+    for load in small + loads:
         load.start()
+    for load in small:
+        load.wait()
     for s in range(slots):
         request = jnp.maximum(owner_ref[0, s], 0)
         begin = len_ref[request] - owner_ref[1, s] * piece_rows
@@ -536,7 +622,6 @@
     columns = queries.shape[2]
     reqs = 16
     half = reqs * tree_size // 2
-    smem = pl.BlockSpec(memory_space=pltpu.SMEM)
     vmem = pl.BlockSpec(memory_space=pltpu.VMEM)
     hbm = pl.BlockSpec(memory_space=pltpu.HBM)
     pieces = reqs * (slots + 1)
@@ -553,6 +638,7 @@
         out_specs=(vmem, vmem),
         scratch_shapes=[
             pltpu.SMEM(owner_t.shape, i32),
+            pltpu.VMEM(owner_t.shape, i32),
             pltpu.SMEM(cache_len.shape, i32),
             pltpu.VMEM(tree_parent.shape, i32),
             pltpu.VMEM(path_t.shape, i32),
@@ -560,8 +646,12 @@
             pltpu.VMEM(tree_kv.shape, bf16),
             pltpu.VMEM(cache_kv.shape, bf16),
             pltpu.VMEM(out_weight.shape, bf16),
-            pltpu.VMEM((reqs, PAD, columns // 2), bf16),
-            pltpu.VMEM((reqs, PAD, columns // 2), bf16),
+            pltpu.VMEM((reqs, PAD, HD), bf16),
+            pltpu.VMEM((reqs, PAD, HD), bf16),
+            pltpu.VMEM((reqs, 8, 128), i32),
+            pltpu.SMEM((reqs, 8, 128), i32),
+            pltpu.VMEM((reqs - 1, slots * PAD, HD), bf16),
+            pltpu.VMEM((reqs, slots * PAD, HD), bf16),
             pltpu.VMEM((PAD, columns), f32),
             pltpu.VMEM((PAD, width), f32),
             pltpu.VMEM((PAD, width), bf16),
@@ -575,9 +665,13 @@
             pltpu.VMEM((2, reqs, half, HD), bf16),
             pltpu.VMEM((half, out_weight.shape[1]), bf16),
             pltpu.VMEM((half, out_weight.shape[1]), bf16),
-            dma((8,)),
-            dma((2, KINDS)),
-            dma((2, KINDS)),
+            dma((10,)),
+            dma((reqs,)),
+            dma((reqs,)),
+            dma((reqs,)),
+            dma((reqs,)),
+            dma((reqs,)),
+            dma((reqs,)),
             dma((4, 4)),
             dma((reqs,)),
             dma((2, KINDS)),
@@ -592,9 +686,16 @@
     cache_out = pl.pallas_call(
         append_kernel,
         out_shape=jax.ShapeDtypeStruct(cache_kv.shape, bf16),
-        in_specs=[smem, smem, smem, hbm, vmem],
+        in_specs=[hbm] * 5,
         out_specs=hbm,
-        scratch_shapes=[dma((2 * slots,))] + [pltpu.VMEM(cache_kv.shape[1:], bf16)] * slots,
+        scratch_shapes=[
+            pltpu.SMEM(owner_t.shape, i32),
+            pltpu.SMEM(cache_len.shape, i32),
+            pltpu.SMEM(path_t.shape, i32),
+            pltpu.VMEM((slots, 16, columns), bf16),
+            dma((2 * slots + 4,)),
+        ]
+        + [pltpu.VMEM(cache_kv.shape[1:], bf16)] * slots,
         compiler_params=pltpu.CompilerParams(vmem_limit_bytes=VMEM_LIMIT),
     )(owner_t, cache_len, path_t, cache_kv, rows)
     mixed = mixed.reshape(tree_size, reqs // 2, out_weight.shape[1]).transpose(1, 0, 2)

time: 70.7 us -> 65.9 us (0.932)
  Pallas kernels: 69.2 us -> 64.4 us
    pallas_call x1, Pallas kernels: 65.9 us -> 61.9 us  [shards_grid(): pl.pallas_call(layer_kernel, out_shape=(jax.ShapeDtypeStruct((half, out_w...]
    pallas_call x1, Pallas kernels: 3.29 us -> 2.47 us  [shards_grid(): pl.pallas_call(append_kernel, out_shape=jax.ShapeDtypeStruct(cache_kv.sha...]
where the time goes in v4:
time: 65.9 us; the launch traced here: 65.7 us
  Pallas kernels  64.4 us (98%)
  between operations  0.66 us (1%)
    pallas_call x1, Pallas kernels, shards_grid(): pl.pallas_call(layer_kernel, out_shape=(jax.ShapeDtypeStruct((half, out_w...  61.9 us
    pallas_call x1, Pallas kernels, shards_grid(): pl.pallas_call(append_kernel, out_shape=jax.ShapeDtypeStruct(cache_kv.sha...  2.47 us

profile of v4, /device:TPU:0, one launch (start us, length us, event | category | flops | bytes accessed | tf_op | source)
XLA Modules:
  0.0 65.7 jit_solution(7199946868924977726)
XLA Ops:
  0.6 61.9 %shard_map.95 = (bf16[224,256]{1,0:T(8,128)(2,1)}, bf16[3,16,2048]{2,1,0:T(8,128)(2,1)}) custom-call(s32[2,3]{1,0:T(2,128)} %bitcast.8, s32[16]{0:T(128)} %len_h.3, s32[1,28]{1,0:T(1,128)} %parent_h.1, s32[8,16]{1,0:T(8,128)} %bitcast.6, bf16[1,28,2048]{2,1,0:T(8,128)(2,1)} %query_h.1, bf16[1,28,1024]{2,1,0:T(8,128)(2,1)} %tree_h.1, ...), custom_call_target="tpu_custom_call" | custom-call | tf_op jit(solution)/shard_map/pallas_call | solution.py:631
  62.6 0.0 copy-start
  62.6 2.5 %shard_map.96 = bf16[3,256,1024]{2,1,0:T(8,128)(2,1)} custom-call(s32[2,3]{1,0:T(2,128)} %bitcast.9, s32[16]{0:T(128)} %len_h.3, s32[8,16]{1,0:T(8,128)} %bitcast.7, bf16[3,256,1024]{2,1,0:T(8,128)(2,1)} %cache_ref.1, bf16[3,16,2048]{2,1,0:T(8,128)(2,1)} %get-tuple-element.5.rows_h), custom_call_target="tpu_custom_call" | custom-call | tf_op jit(solution)/shard_map/pallas_call | solution.py:686
  65.1 0.0 copy-done
  65.1 0.6 copy.11
Async XLA Ops:
  62.6 2.5 %copy-start = (bf16[224,256]{1,0:T(8,128)(2,1)S(1)}, bf16[224,256]{1,0:T(8,128)(2,1)}, u32[]{:S(2)}) copy-start(bf16[224,256]{1,0:T(8,128)(2,1)} %get-tuple-element.4) | copy-start | bytes 344068

commit v5 on v4

--- a/solution.py
+++ b/solution.py
@@ -280,9 +280,9 @@
     owner_h, len_h, parent_h, path_h, query_h, tree_h, cache_h, weight_h,
     mixed_ref, rows_ref,
     owner_ref, owner_v, len_ref, parent_ref, path_ref, query_ref, tree_ref, cache_v, weight_v,
-    own_heads, owned, known_v, known, staged, asked, packed, tree_f, tree_b, reach_v, outgoing, incoming,
+    own_heads, owned, known_v, known, staged, asked, packed, tree_f, tree_b, reach_v, outgoing, incoming, tree_out, tree_in,
     wide, owners, joined, compact, attn, half_out, half_in,
-    local_sem, send0, recv0, send5, recv5, send1, recv1, send2, recv2, send3, recv3, send4, recv4,
+    local_sem, send0, recv0, send5, recv5, send6, recv6, send1, recv1, send2, recv2, send3, recv3, send4, recv4,
 ):
     me, y, x, planes = place()
     tp = lax.axis_index("tp")
@@ -378,6 +378,15 @@
         short = reached.astype(jnp.bfloat16)
         reached = jnp.minimum(jnp.dot(short, short, preferred_element_type=jnp.float32), 1.0)
     tree_mask = jnp.concatenate([reached] * 4, axis=0) > 0.5
+    for kv in range(4):
+        query = jnp.concatenate([own_heads[4 * g + kv] for g in range(4)], axis=0)
+        at = kv * 2 * HD
+        blocks = attend(
+            query, tree_b[:, at : at + HD], tree_b[:, at + HD : at + 2 * HD], tree_mask, scaling,
+            me.astype(jnp.float32),
+        )
+        for g in range(4):
+            tree_out[4 * g + kv] = blocks[g]
     for load in loads[4:7]:
         load.wait()
     for source in others:
@@ -397,6 +406,9 @@
         stage(target, staged.at[n])
         post(staged.at[n], asked.at[me], target, send5, recv5, n)
     stage(me, asked.at[me])
+    for n, target in enumerate(others):
+        post(tree_out.at[target], tree_in.at[me], target, send6, recv6, n)
+    tree_in[me] = tree_out[me]
 
     sent = []
 
@@ -408,17 +420,13 @@
             def _():
                 take(asked.at[source], send5, recv5, source)
 
-        for s in range(slots + 1):
-            if s < slots:
-                owner = owner_ref[0, s]
-                request = jnp.maximum(owner, 0)
-                limit = jnp.where(owner >= 0, len_ref[request] - owner_ref[1, s] * piece_rows, 0)
-                mask = iota((4 * PAD, piece_rows), 1) < limit
-                keys = cache_v.at[s]
-                parts = [asked[4 * g + kv, s * PAD : (s + 1) * PAD, :] for g in range(4)]
-            else:
-                owner, keys, mask = me, tree_b, tree_mask
-                parts = [own_heads[4 * g + kv] for g in range(4)]
+        for s in range(slots):
+            owner = owner_ref[0, s]
+            request = jnp.maximum(owner, 0)
+            limit = jnp.where(owner >= 0, len_ref[request] - owner_ref[1, s] * piece_rows, 0)
+            mask = iota((4 * PAD, piece_rows), 1) < limit
+            keys = cache_v.at[s]
+            parts = [asked[4 * g + kv, s * PAD : (s + 1) * PAD, :] for g in range(4)]
             query = jnp.concatenate(parts, axis=0)
             at = kv * 2 * HD
             blocks = attend(
@@ -475,7 +483,11 @@
         ).wait_recv()
 
     pieces = 16 * (slots + 1)
-    wide[...] = incoming[...].astype(jnp.float32).reshape(pieces * PAD, HD)
+    for source in others:
+        take(tree_in.at[source], send6, recv6, source)
+    held = 16 * slots
+    wide[0 : held * PAD] = incoming[...].astype(jnp.float32).reshape(held * PAD, HD)
+    wide[held * PAD :] = tree_in[...].astype(jnp.float32).reshape(16 * PAD, HD)
     level = wide[pl.ds(28, pieces, stride=PAD), :] + wide[pl.ds(29, pieces, stride=PAD), :]
     holder = wide[pl.ds(30, pieces, stride=PAD), :]
     owners[...] = holder
@@ -494,13 +506,12 @@
         def join(i, carry):
             r = part * 8 + i
             mine = r.astype(jnp.float32)
-            first_row = pl.multiple_of((r * (slots + 1) + slots) * PAD, PAD)
+            first_row = pl.multiple_of((held + r) * PAD, PAD)
             total = wide[pl.ds(first_row, PAD), :]
-            for b in range(pieces):
-                if b % (slots + 1) < slots:
-                    total = total + jnp.where(
-                        owners[b : b + 1] == mine, wide[b * PAD : (b + 1) * PAD], 0.0
-                    )
+            for b in range(held):
+                total = total + jnp.where(
+                    owners[b : b + 1] == mine, wide[b * PAD : (b + 1) * PAD], 0.0
+                )
             joined[i] = total
             return carry
 
@@ -648,16 +659,18 @@
             pltpu.VMEM(out_weight.shape, bf16),
             pltpu.VMEM((reqs, PAD, HD), bf16),
             pltpu.VMEM((reqs, PAD, HD), bf16),
-            pltpu.VMEM((reqs, 8, 128), i32),
-            pltpu.SMEM((reqs, 8, 128), i32),
+            pltpu.VMEM((reqs, 1, 128), i32),
+            pltpu.SMEM((reqs, 1, 128), i32),
             pltpu.VMEM((reqs - 1, slots * PAD, HD), bf16),
             pltpu.VMEM((reqs, slots * PAD, HD), bf16),
             pltpu.VMEM((PAD, columns), f32),
             pltpu.VMEM((PAD, width), f32),
             pltpu.VMEM((PAD, width), bf16),
             pltpu.VMEM((PAD, PAD), f32),
-            pltpu.VMEM((4, 4, (slots + 1) * PAD, HD), bf16),
-            pltpu.VMEM((reqs, (slots + 1) * PAD, HD), bf16),
+            pltpu.VMEM((4, 4, slots * PAD, HD), bf16),
+            pltpu.VMEM((reqs, slots * PAD, HD), bf16),
+            pltpu.VMEM((reqs, PAD, HD), bf16),
+            pltpu.VMEM((reqs, PAD, HD), bf16),
             pltpu.VMEM((pieces * PAD, HD), f32),
             pltpu.VMEM((pieces, HD), f32),
             pltpu.VMEM((reqs // 2, PAD, HD), f32),
@@ -666,6 +679,8 @@
             pltpu.VMEM((half, out_weight.shape[1]), bf16),
             pltpu.VMEM((half, out_weight.shape[1]), bf16),
             dma((10,)),
+            dma((reqs,)),
+            dma((reqs,)),
             dma((reqs,)),
             dma((reqs,)),
             dma((reqs,)),

time: 65.9 us -> 65 us (0.986)
  Pallas kernels: 64.4 us -> 63.5 us
    pallas_call x1, Pallas kernels: 61.9 us -> 61.1 us  [shards_grid(): pl.pallas_call(layer_kernel, out_shape=(jax.ShapeDtypeStruct((half, out_w...]
where the time goes in v5:
time: 65 us; the launch traced here: 64.9 us
  Pallas kernels  63.5 us (98%)
  between operations  0.66 us (1%)
  local copies, waits for them, and re-layouts  0.65 us (1%)
    pallas_call x1, Pallas kernels, shards_grid(): pl.pallas_call(layer_kernel, out_shape=(jax.ShapeDtypeStruct((half, out_w...  61.1 us
    pallas_call x1, Pallas kernels, shards_grid(): pl.pallas_call(append_kernel, out_shape=jax.ShapeDtypeStruct(cache_kv.sha...  2.47 us

profile of v5, /device:TPU:0, one launch (start us, length us, event | category | flops | bytes accessed | tf_op | source)
XLA Modules:
  0.0 64.9 jit_solution(10745309868304930355)
XLA Ops:
  0.6 61.1 %shard_map.95 = (bf16[224,256]{1,0:T(8,128)(2,1)}, bf16[3,16,2048]{2,1,0:T(8,128)(2,1)}) custom-call(s32[2,3]{1,0:T(2,128)} %bitcast.8, s32[16]{0:T(128)} %len_h.3, s32[1,28]{1,0:T(1,128)} %parent_h.1, s32[8,16]{1,0:T(8,128)} %bitcast.6, bf16[1,28,2048]{2,1,0:T(8,128)(2,1)} %query_h.1, bf16[1,28,1024]{2,1,0:T(8,128)(2,1)} %tree_h.1, ...), custom_call_target="tpu_custom_call" | custom-call | tf_op jit(solution)/shard_map/pallas_call | solution.py:642
  61.7 0.0 copy-start
  61.7 2.5 %shard_map.96 = bf16[3,256,1024]{2,1,0:T(8,128)(2,1)} custom-call(s32[2,3]{1,0:T(2,128)} %bitcast.9, s32[16]{0:T(128)} %len_h.3, s32[8,16]{1,0:T(8,128)} %bitcast.7, bf16[3,256,1024]{2,1,0:T(8,128)(2,1)} %cache_ref.1, bf16[3,16,2048]{2,1,0:T(8,128)(2,1)} %get-tuple-element.5.rows_h), custom_call_target="tpu_custom_call" | custom-call | tf_op jit(solution)/shard_map/pallas_call | solution.py:701
  64.2 0.0 copy-done
  64.2 0.6 copy.11
Async XLA Ops:
  61.7 2.5 %copy-start = (bf16[224,256]{1,0:T(8,128)(2,1)S(1)}, bf16[224,256]{1,0:T(8,128)(2,1)}, u32[]{:S(2)}) copy-start(bf16[224,256]{1,0:T(8,128)(2,1)} %get-tuple-element.4) | copy-start | bytes 344068

commit v6 on v5

--- a/solution.py
+++ b/solution.py
@@ -196,25 +196,25 @@
     def begin(self):
         self.go(self.me, "all", self.column[1], 0, 0)
         self.relay(self.me, "all", self.middle, 1, 1)
-        self.step(0)
-
-    def step(self, k):
+        self.along(0)
+
+    def along(self, k):
         column = self.column
-        if k < 4:
-            if k:
-                self.copy(column[k], "all", self.near_x, k - 1).wait_recv()
-                if k == 1:
-                    self.relay(column[1], "all", self.middle, 2, 2)
-                else:
-                    self.relay(column[k], "all", column[1], k + 1, k - 1)
-            self.go(column[k], "all", self.near_x, 5 + k)
-            self.go(column[k], "all", self.near_y, 9 + k)
         if k:
-            across_x, across_y = column[k - 1] + self.to_x, column[k - 1] + self.to_y
-            self.copy(across_x, "all", self.near_x, 4 + k).wait_recv()
-            self.go(across_x, "top", self.near_y, 12 + k)
-            self.copy(across_y, "all", self.near_x, 8 + k).wait_recv()
-            self.go(across_y, "low", self.near_x, 16 + k)
+            self.copy(column[k], "all", self.near_x, k - 1).wait_recv()
+            if k == 1:
+                self.relay(column[1], "all", self.middle, 2, 2)
+            else:
+                self.relay(column[k], "all", column[1], k + 1, k - 1)
+        self.go(column[k], "all", self.near_x, 5 + k)
+        self.go(column[k], "all", self.near_y, 9 + k)
+
+    def across(self, k):
+        across_x, across_y = self.column[k] + self.to_x, self.column[k] + self.to_y
+        self.copy(across_x, "all", self.near_x, 5 + k).wait_recv()
+        self.go(across_x, "top", self.near_y, 13 + k)
+        self.copy(across_y, "all", self.near_x, 9 + k).wait_recv()
+        self.go(across_y, "low", self.near_x, 17 + k)
 
     def end(self):
         for k in range(4):
@@ -524,14 +524,20 @@
     join_half(1 - tp, 0)
     last[0].begin()
     join_half(tp, 1)
-    last[0].step(1)
     last[1].begin()
-    last[0].step(2)
-    last[1].step(1)
-    last[0].step(3)
-    last[1].step(2)
-    last[0].step(4)
-    last[1].step(3)
+    last[0].along(1)
+    last[1].along(1)
+    last[0].across(0)
+    last[0].along(2)
+    last[1].across(0)
+    last[1].along(2)
+    last[0].across(1)
+    last[0].along(3)
+    last[1].across(1)
+    last[1].along(3)
+    last[0].across(2)
+    last[0].across(3)
+    last[1].across(2)
     loads[7].wait()
 
     def project(part):
@@ -549,7 +555,7 @@
         return total
 
     last[0].end()
-    last[1].step(4)
+    last[1].across(3)
     half_out[...] = project(0).astype(jnp.bfloat16)
     swap = pltpu.make_async_remote_copy(
         src_ref=half_out,

time: 65 us -> 62.6 us (0.963)
  Pallas kernels: 63.5 us -> 61.1 us
    pallas_call x1, Pallas kernels: 61.1 us -> 58.6 us  [shards_grid(): pl.pallas_call(layer_kernel, out_shape=(jax.ShapeDtypeStruct((half, out_w...]
where the time goes in v6:
time: 62.6 us; the launch traced here: 62.4 us
  Pallas kernels  61.1 us (98%)
  between operations  0.66 us (1%)
  local copies, waits for them, and re-layouts  0.65 us (1%)
    pallas_call x1, Pallas kernels, shards_grid(): pl.pallas_call(layer_kernel, out_shape=(jax.ShapeDtypeStruct((half, out_w...  58.6 us
    pallas_call x1, Pallas kernels, shards_grid(): pl.pallas_call(append_kernel, out_shape=jax.ShapeDtypeStruct(cache_kv.sha...  2.47 us

profile of v6, /device:TPU:0, one launch (start us, length us, event | category | flops | bytes accessed | tf_op | source)
XLA Modules:
  0.0 62.4 jit_solution(4153837542180554072)
XLA Ops:
  0.6 58.6 %shard_map.95 = (bf16[224,256]{1,0:T(8,128)(2,1)}, bf16[3,16,2048]{2,1,0:T(8,128)(2,1)}) custom-call(s32[2,3]{1,0:T(2,128)} %bitcast.8, s32[16]{0:T(128)} %len_h.3, s32[1,28]{1,0:T(1,128)} %parent_h.1, s32[8,16]{1,0:T(8,128)} %bitcast.6, bf16[1,28,2048]{2,1,0:T(8,128)(2,1)} %query_h.1, bf16[1,28,1024]{2,1,0:T(8,128)(2,1)} %tree_h.1, ...), custom_call_target="tpu_custom_call" | custom-call | tf_op jit(solution)/shard_map/pallas_call | solution.py:648
  59.2 0.0 copy-start
  59.3 2.5 %shard_map.96 = bf16[3,256,1024]{2,1,0:T(8,128)(2,1)} custom-call(s32[2,3]{1,0:T(2,128)} %bitcast.9, s32[16]{0:T(128)} %len_h.3, s32[8,16]{1,0:T(8,128)} %bitcast.7, bf16[3,256,1024]{2,1,0:T(8,128)(2,1)} %cache_ref.1, bf16[3,16,2048]{2,1,0:T(8,128)(2,1)} %get-tuple-element.5.rows_h), custom_call_target="tpu_custom_call" | custom-call | tf_op jit(solution)/shard_map/pallas_call | solution.py:707
  61.7 0.0 copy-done
  61.7 0.6 %copy.11 = bf16[8,28,256]{2,0,1:T(8,128)(2,1)} copy(bf16[8,28,256]{2,0,1:T(8,128)(2,1)S(1)} %bitcast.5) | data formatting | bytes 229376
Async XLA Ops:
  59.2 2.5 %copy-start = (bf16[224,256]{1,0:T(8,128)(2,1)S(1)}, bf16[224,256]{1,0:T(8,128)(2,1)}, u32[]{:S(2)}) copy-start(bf16[224,256]{1,0:T(8,128)(2,1)} %get-tuple-element.4) | copy-start | bytes 344068
